TPU v7x, 32 devices: a whole 2x2x4 slice. The times are simulated.
32 devices in a mesh: ctx: 8 (over y, x, core), req: 4 (over z).
Axes of the slice: x: 2, y: 2, z: 4, core: 2. Of those that a mesh axis runs over, the one named last changes fastest.
Arguments:
- queries: bfloat16 [2048, 2048], P(('ctx', 'req')), may hold values from -20 to 20
- q_pos: int32 [2048], P(('ctx', 'req')), may hold values from 1 to 18431
- req_of: int32 [2048, 1], P(('ctx', 'req')), may hold values from 0 to 3; in each aligned block of 64 rows (0 to 63, 64 to 127, ...) at most 20 rows name the same one
- cache: bfloat16 [4, 18432, 256], P('req', 'ctx'), may hold values from -6 to 6
- cache_len: int32 [4], replicated, may hold values from 2 to 18432
Outputs:
- attended: bfloat16 [2048, 2048], P(('ctx', 'req'))
Inputs may be any that keep to these rules, and one draw needn't show every extreme that they name: `req_of`: no more than 20 of one device's 64 tokens name the same request, and some device's tokens reach 20 for some request.
All inputs are finite; a program needn't handle non-finite values.
Results may differ from a plain program's by a relative error of at most 0.006.
Values may be sent and summed in bfloat16 or wider, within the bound.
No kernel may reach another device: no remote copies, remote signals or barrier semaphores. Data moves between devices by JAX's collectives and lax.ppermute only.
A program may use at most 128 MiB of HBM per device.

v0:
```python
import jax
import jax.numpy as jnp
from jax import lax
from jax.sharding import PartitionSpec as P

H = 16
HD = 128


def shifted(block, axis, distance):
    devices = range(lax.axis_size(axis))
    route = [((i - distance) % len(devices), i) for i in devices]
    return lax.ppermute(block, axis, route)


def shard_partial(query, positions, span, key_start, length):
    slot_rows = query.shape[0]
    keys = span[:, :HD]
    values = span[:, HD:]
    scores = jnp.einsum("shd,kd->shk", query, keys, preferred_element_type=jnp.float32) * HD ** (
        -0.5
    )
    key_pos = key_start + jnp.arange(span.shape[0], dtype=jnp.int32)
    live = (key_pos[None, :] < length) & (key_pos[None, :] <= positions[:, None])
    live3 = live[:, None, :]
    scores = jnp.where(live3, scores, jnp.float32(-1e30))
    top = jnp.max(scores, axis=-1)
    weights = jnp.where(live3, jnp.exp(scores - top[..., None]), jnp.float32(0.0))
    total = jnp.sum(weights, axis=-1)
    safe = jnp.where(total > 0.0, total, jnp.float32(1.0))
    summed = jnp.einsum(
        "shk,kd->shd", weights.astype(jnp.bfloat16), values, preferred_element_type=jnp.float32
    )
    partial_out = (summed / safe[..., None]).reshape(slot_rows, H * HD).astype(jnp.bfloat16)
    lse = jnp.where(total > 0.0, top + jnp.log(safe), jnp.float32(-1e30))
    return (partial_out, lse)


def merge_parts(part_buf, lse_buf):
    count = part_buf.shape[0]
    slot_rows = part_buf.shape[1]
    high = jnp.max(lse_buf, axis=0)
    share = jnp.exp(lse_buf - high[None])
    widened = part_buf.reshape(count, slot_rows, H, HD).astype(jnp.float32)
    merged = jnp.sum(share[..., None] * widened, axis=0) / jnp.sum(share, axis=0)[..., None]
    return merged.reshape(slot_rows, H * HD).astype(jnp.bfloat16)


def per_device(queries, q_pos, req_of, cache, cache_len):
    tok_rows = queries.shape[0]
    groups = lax.axis_size("req")
    capacity = 5 * tok_rows // (4 * groups)
    slot_rows = groups * capacity
    shard_len = cache.shape[1]
    target = req_of[:, 0]
    onehot = (target[:, None] == jnp.arange(groups, dtype=jnp.int32)[None, :]).astype(jnp.int32)
    before = jnp.cumsum(onehot, axis=0) - onehot
    rank = jnp.sum(before * onehot, axis=1)
    slot = target * capacity + rank
    send_q = jnp.zeros((slot_rows, H * HD), jnp.bfloat16).at[slot].set(queries)
    send_pos = jnp.full((slot_rows,), -1, jnp.int32).at[slot].set(q_pos)
    recv_q, recv_pos = (
        lax.all_to_all(
            send_q.reshape(groups, capacity, H * HD), "req", split_axis=0, concat_axis=0, tiled=True
        ),
        lax.all_to_all(
            send_pos.reshape(groups, capacity), "req", split_axis=0, concat_axis=0, tiled=True
        ),
    )
    query = recv_q.reshape(slot_rows, H, HD)
    positions = recv_pos.reshape(slot_rows)
    length = lax.dynamic_index_in_dim(cache_len, lax.axis_index("req"), 0, keepdims=False)
    cycle = lax.axis_size("ctx")
    empty_parts = jnp.zeros((cycle, slot_rows, H * HD), jnp.bfloat16)
    empty_lse = jnp.full((cycle, slot_rows, H), -1e30, jnp.float32)
    here = lax.axis_index("ctx")
    home_start = here * shard_len
    span = cache[0]
    first_part, first_lse = shard_partial(query, positions, span, home_start, length)
    part_buf = lax.dynamic_update_slice_in_dim(empty_parts, first_part[None], here, 0)
    lse_buf = lax.dynamic_update_slice_in_dim(empty_lse, first_lse[None], here, 0)

    def one_turn(turn, carry):
        visiting, visit_pos, parts_in, lses_in = carry
        visiting, visit_pos = shifted((visiting, visit_pos), "ctx", 1)
        anchor = (here - turn) % cycle
        part_out, lse = shard_partial(visiting, visit_pos, span, home_start, length)
        parts_in = lax.dynamic_update_slice_in_dim(parts_in, part_out[None], anchor, 0)
        lses_in = lax.dynamic_update_slice_in_dim(lses_in, lse[None], anchor, 0)
        return (visiting, visit_pos, parts_in, lses_in)

    final = lax.fori_loop(1, cycle, one_turn, (query, positions, part_buf, lse_buf))
    part_buf, lse_buf = (
        lax.all_to_all(final[2], "ctx", split_axis=0, concat_axis=0, tiled=True),
        lax.all_to_all(
            final[3].astype(jnp.bfloat16), "ctx", split_axis=0, concat_axis=0, tiled=True
        ).astype(jnp.float32),
    )
    output = merge_parts(part_buf, lse_buf).reshape(groups, capacity, H * HD)
    back = lax.all_to_all(output, "req", split_axis=0, concat_axis=0, tiled=True).reshape(
        slot_rows, H * HD
    )
    return back[slot]


def solution(mesh):
    in_specs = (
        P(("ctx", "req"), None),
        P(("ctx", "req")),
        P(("ctx", "req"), None),
        P("req", "ctx", None),
        P(),
    )
    out_specs = P(("ctx", "req"), None)
    return jax.shard_map(
        per_device, mesh=mesh, in_specs=in_specs, out_specs=out_specs, check_vma=False
    )
```

profile of v0, /device:TPU:0, one launch (start us, length us, event | category | flops | bytes accessed | tf_op | source)
XLA Modules:
  0.0 232.2 jit_solution(2054452210117746999)
XLA Ops:
  3.9 6.3 %all-to-all-start.1 = ((s32[4,1,20]{2,1,0:T(1,128)}), s32[4,1,20]{2,1,0:T(1,128)S(1)}, u32[]{:S(2)}, u32[]{:S(2)}) async-start(s32[4,1,20]{2,1,0:T(1,128)} %bitcast.7), calls=%async_computation.1 | async-start | bytes 4096 | tf_op jit(solution)/shard_map/all_to_all | solution.py:66
  15.7 4.0 %all-to-all-start = ((bf16[4,20,2048]{2,1,0:T(8,128)(2,1)}), bf16[4,20,2048]{2,1,0:T(8,128)(2,1)S(1)}, u32[]{:S(2)}, u32[]{:S(2)}) async-start(bf16[4,20,2048]{2,1,0:T(8,128)(2,1)} %reshape.229), calls=%async_computation | async-start | bytes 786432 | tf_op jit(solution)/shard_map/all_to_all | solution.py:63
  21.1 9.7 %all-to-all-done = bf16[4,20,2048]{2,1,0:T(8,128)(2,1)S(1)} async-done(((bf16[4,20,2048]{2,1,0:T(8,128)(2,1)}), bf16[4,20,2048]{2,1,0:T(8,128)(2,1)S(1)}, u32[]{:S(2)}, u32[]{:S(2)}) %all-to-all-start) | async-done | bytes 327712 | tf_op jit(solution)/shard_map/all_to_all | solution.py:63
  31.0 4.0 %fusion.23 = (f32[80,16]{1,0:T(8,128)S(1)}, f32[80,16,2304]{2,1,0:T(8,128)S(1)}) fusion(pred[80,2304]{1,0:T(8,128)(4,1)S(1)} %compare_and_fusion.1, bf16[80,16,128]{2,1,0:T(8,128)(2,1)S(1)} %reshape.230, bf16[2304,256]{1,0:T(8,128)(2,1)} %bitcast.48), kind=kOutput, calls=%fused_computation.32 | convolution fusion | flops 763820800 | bytes 12903424 | tf_op jit(solution)/shard_map/shd,kd->shk/dot_general | solution.py:20
  35.0 3.8 %fusion.24 = f32[80,16]{1,0:T(8,128)S(1)} fusion(f32[80,16,2304]{2,1,0:T(8,128)S(1)} %get-tuple-element.252, f32[80,16]{1,0:T(8,128)S(1)} %get-tuple-element.251, pred[80,2304]{1,0:T(8,128)(4,1)S(1)} %compare_and_fusion.1), kind=kLoop, calls=%fused_computation.33 | loop fusion | flops 14744320 | bytes 11991040 | tf_op jit(solution)/shard_map/reduce_sum | solution.py:29
  44.0 124.6 %while.21 = (s32[]{:T(128)}, bf16[80,16,128]{2,1,0:T(8,128)(2,1)S(1)}, s32[80]{0:T(128)S(1)}, bf16[8,80,2048]{2,1,0:T(8,128)(2,1)}, bf16[8,80,16]{2,1,0:T(8,128)...) while((s32[]{:T(128)}, ...), condition=%wide.region_9.10_spmd, body=%wide.region_6.9_spmd.sunk | while | flops 1548996352 | bytes 41494580 | solution.py:92
  48.1 3.4 %collective-permute-done = bf16[80,16,128]{2,1,0:T(8,128)(2,1)S(1)} collective-permute-done((bf16[80,16,128]{2,1,0:T(8,128)(2,1)S(1)}, bf16[80,16,128]{2,1,0:T(8,128)(2,1)S(1)}, u32[]{:S(2)}, u32[]{:S(2)}) %collective-permute-start) | collective-permute-done | bytes 327712 | tf_op jit(solution)/shard_map/while/body/eval_jaxpr/ppermute | solution.py:13
  53.9 3.8 %fusion.62 = f32[80,16]{1,0:T(8,128)S(1)} fusion(f32[80,16,2304]{2,1,0:T(8,128)S(1)} %get-tuple-element.310, f32[80,16]{1,0:T(8,128)S(1)} %get-tuple-element.311, pred[80,2304]{1,0:T(8,128)(4,1)S(1)} %compare_and_fusion.3), kind=kLoop, calls=%fused_computation.6.clone.1 | loop fusion | flops 14744320 | bytes 11991040 | tf_op jit(solution)/shard_map/while/body/eval_jaxpr/reduce_sum | solution.py:29
  65.9 3.4 %collective-permute-done = bf16[80,16,128]{2,1,0:T(8,128)(2,1)S(1)} collective-permute-done((bf16[80,16,128]{2,1,0:T(8,128)(2,1)S(1)}, bf16[80,16,128]{2,1,0:T(8,128)(2,1)S(1)}, u32[]{:S(2)}, u32[]{:S(2)}) %collective-permute-start) | collective-permute-done | bytes 327712 | tf_op jit(solution)/shard_map/while/body/eval_jaxpr/ppermute | solution.py:13
  71.8 3.8 %fusion.62 = f32[80,16]{1,0:T(8,128)S(1)} fusion(f32[80,16,2304]{2,1,0:T(8,128)S(1)} %get-tuple-element.310, f32[80,16]{1,0:T(8,128)S(1)} %get-tuple-element.311, pred[80,2304]{1,0:T(8,128)(4,1)S(1)} %compare_and_fusion.3), kind=kLoop, calls=%fused_computation.6.clone.1 | loop fusion | flops 14744320 | bytes 11991040 | tf_op jit(solution)/shard_map/while/body/eval_jaxpr/reduce_sum | solution.py:29
  80.4 3.0 %collective-permute-done.1 = s32[80]{0:T(128)S(1)} collective-permute-done((s32[80]{0:T(128)S(1)}, s32[80]{0:T(128)S(1)}, u32[]{:S(2)}, u32[]{:S(2)}) %collective-permute-start.1) | collective-permute-done | bytes 352 | tf_op jit(solution)/shard_map/while/body/eval_jaxpr/ppermute | solution.py:13
  83.7 3.4 %collective-permute-done = bf16[80,16,128]{2,1,0:T(8,128)(2,1)S(1)} collective-permute-done((bf16[80,16,128]{2,1,0:T(8,128)(2,1)S(1)}, bf16[80,16,128]{2,1,0:T(8,128)(2,1)S(1)}, u32[]{:S(2)}, u32[]{:S(2)}) %collective-permute-start) | collective-permute-done | bytes 327712 | tf_op jit(solution)/shard_map/while/body/eval_jaxpr/ppermute | solution.py:13
  89.6 3.8 %fusion.62 = f32[80,16]{1,0:T(8,128)S(1)} fusion(f32[80,16,2304]{2,1,0:T(8,128)S(1)} %get-tuple-element.310, f32[80,16]{1,0:T(8,128)S(1)} %get-tuple-element.311, pred[80,2304]{1,0:T(8,128)(4,1)S(1)} %compare_and_fusion.3), kind=kLoop, calls=%fused_computation.6.clone.1 | loop fusion | flops 14744320 | bytes 11991040 | tf_op jit(solution)/shard_map/while/body/eval_jaxpr/reduce_sum | solution.py:29
  98.2 3.0 %collective-permute-done.1 = s32[80]{0:T(128)S(1)} collective-permute-done((s32[80]{0:T(128)S(1)}, s32[80]{0:T(128)S(1)}, u32[]{:S(2)}, u32[]{:S(2)}) %collective-permute-start.1) | collective-permute-done | bytes 352 | tf_op jit(solution)/shard_map/while/body/eval_jaxpr/ppermute | solution.py:13
  101.4 3.4 %collective-permute-done = bf16[80,16,128]{2,1,0:T(8,128)(2,1)S(1)} collective-permute-done((bf16[80,16,128]{2,1,0:T(8,128)(2,1)S(1)}, bf16[80,16,128]{2,1,0:T(8,128)(2,1)S(1)}, u32[]{:S(2)}, u32[]{:S(2)}) %collective-permute-start) | collective-permute-done | bytes 327712 | tf_op jit(solution)/shard_map/while/body/eval_jaxpr/ppermute | solution.py:13
  107.4 3.8 %fusion.62 = f32[80,16]{1,0:T(8,128)S(1)} fusion(f32[80,16,2304]{2,1,0:T(8,128)S(1)} %get-tuple-element.310, f32[80,16]{1,0:T(8,128)S(1)} %get-tuple-element.311, pred[80,2304]{1,0:T(8,128)(4,1)S(1)} %compare_and_fusion.3), kind=kLoop, calls=%fused_computation.6.clone.1 | loop fusion | flops 14744320 | bytes 11991040 | tf_op jit(solution)/shard_map/while/body/eval_jaxpr/reduce_sum | solution.py:29
  116.0 3.0 %collective-permute-done.1 = s32[80]{0:T(128)S(1)} collective-permute-done((s32[80]{0:T(128)S(1)}, s32[80]{0:T(128)S(1)}, u32[]{:S(2)}, u32[]{:S(2)}) %collective-permute-start.1) | collective-permute-done | bytes 352 | tf_op jit(solution)/shard_map/while/body/eval_jaxpr/ppermute | solution.py:13
  119.3 3.4 %collective-permute-done = bf16[80,16,128]{2,1,0:T(8,128)(2,1)S(1)} collective-permute-done((bf16[80,16,128]{2,1,0:T(8,128)(2,1)S(1)}, bf16[80,16,128]{2,1,0:T(8,128)(2,1)S(1)}, u32[]{:S(2)}, u32[]{:S(2)}) %collective-permute-start) | collective-permute-done | bytes 327712 | tf_op jit(solution)/shard_map/while/body/eval_jaxpr/ppermute | solution.py:13
  125.2 3.8 %fusion.62 = f32[80,16]{1,0:T(8,128)S(1)} fusion(f32[80,16,2304]{2,1,0:T(8,128)S(1)} %get-tuple-element.310, f32[80,16]{1,0:T(8,128)S(1)} %get-tuple-element.311, pred[80,2304]{1,0:T(8,128)(4,1)S(1)} %compare_and_fusion.3), kind=kLoop, calls=%fused_computation.6.clone.1 | loop fusion | flops 14744320 | bytes 11991040 | tf_op jit(solution)/shard_map/while/body/eval_jaxpr/reduce_sum | solution.py:29
  133.8 3.0 %collective-permute-done.1 = s32[80]{0:T(128)S(1)} collective-permute-done((s32[80]{0:T(128)S(1)}, s32[80]{0:T(128)S(1)}, u32[]{:S(2)}, u32[]{:S(2)}) %collective-permute-start.1) | collective-permute-done | bytes 352 | tf_op jit(solution)/shard_map/while/body/eval_jaxpr/ppermute | solution.py:13
  137.1 3.4 %collective-permute-done = bf16[80,16,128]{2,1,0:T(8,128)(2,1)S(1)} collective-permute-done((bf16[80,16,128]{2,1,0:T(8,128)(2,1)S(1)}, bf16[80,16,128]{2,1,0:T(8,128)(2,1)S(1)}, u32[]{:S(2)}, u32[]{:S(2)}) %collective-permute-start) | collective-permute-done | bytes 327712 | tf_op jit(solution)/shard_map/while/body/eval_jaxpr/ppermute | solution.py:13
  143.0 3.8 %fusion.62 = f32[80,16]{1,0:T(8,128)S(1)} fusion(f32[80,16,2304]{2,1,0:T(8,128)S(1)} %get-tuple-element.310, f32[80,16]{1,0:T(8,128)S(1)} %get-tuple-element.311, pred[80,2304]{1,0:T(8,128)(4,1)S(1)} %compare_and_fusion.3), kind=kLoop, calls=%fused_computation.6.clone.1 | loop fusion | flops 14744320 | bytes 11991040 | tf_op jit(solution)/shard_map/while/body/eval_jaxpr/reduce_sum | solution.py:29
  154.9 3.4 %collective-permute-done = bf16[80,16,128]{2,1,0:T(8,128)(2,1)S(1)} collective-permute-done((bf16[80,16,128]{2,1,0:T(8,128)(2,1)S(1)}, bf16[80,16,128]{2,1,0:T(8,128)(2,1)S(1)}, u32[]{:S(2)}, u32[]{:S(2)}) %collective-permute-start) | collective-permute-done | bytes 327712 | tf_op jit(solution)/shard_map/while/body/eval_jaxpr/ppermute | solution.py:13
  160.8 3.8 %fusion.62 = f32[80,16]{1,0:T(8,128)S(1)} fusion(f32[80,16,2304]{2,1,0:T(8,128)S(1)} %get-tuple-element.310, f32[80,16]{1,0:T(8,128)S(1)} %get-tuple-element.311, pred[80,2304]{1,0:T(8,128)(4,1)S(1)} %compare_and_fusion.3), kind=kLoop, calls=%fused_computation.6.clone.1 | loop fusion | flops 14744320 | bytes 11991040 | tf_op jit(solution)/shard_map/while/body/eval_jaxpr/reduce_sum | solution.py:29
  168.7 7.5 %all_to_all.29 = bf16[8,80,16]{1,2,0:T(8,128)(2,1)S(1)} all-to-all(bf16[8,80,16]{1,2,0:T(8,128)(2,1)S(1)} %copy.10), channel_id=1, replica_groups=mesh['ctx'=8,'req'=4] {'ctx'}, dimensions={0} | all-to-all | bytes 40960 | tf_op jit(solution)/shard_map/all_to_all | solution.py:95
  176.2 3.6 %all-to-all-start.3 = ((bf16[8,80,2048]{2,1,0:T(8,128)(2,1)}), bf16[8,80,2048]{2,1,0:T(8,128)(2,1)S(1)}, u32[]{:S(2)}, u32[]{:S(2)}) async-start(bf16[8,80,2048]{2,1,0:T(8,128)(2,1)} %get-tuple-element.228), calls=%async_computation.3 | async-start | bytes 5242880 | tf_op jit(solution)/shard_map/all_to_all | solution.py:94
  180.0 3.5 %mul.42 = f32[8,80,16,128]{3,2,1,0:T(8,128)} broadcast(f32[8,80,16]{2,1,0:T(8,128)S(1)} %copy.11), dimensions={0,1,2} | broadcast | bytes 5283840 | tf_op jit(solution)/shard_map/mul | solution.py:45
  183.5 6.7 %mul.43 = f32[8,80,2048]{2,1,0:T(8,128)} reshape(f32[8,80,16,128]{3,2,1,0:T(8,128)} %mul.42) | data formatting | bytes 10485760 | tf_op jit(solution)/shard_map/mul | solution.py:45
  192.6 19.4 %all-to-all-done.3 = bf16[8,80,2048]{2,1,0:T(8,128)(2,1)S(1)} async-done(((bf16[8,80,2048]{2,1,0:T(8,128)(2,1)}), bf16[8,80,2048]{2,1,0:T(8,128)(2,1)S(1)}, u32[]{:S(2)}, u32[]{:S(2)}) %all-to-all-start.3) | async-done | bytes 2621472 | tf_op jit(solution)/shard_map/all_to_all | solution.py:94
  212.0 4.2 %multiply_reduce_fusion = f32[80,2048]{1,0:T(8,128)} fusion(f32[8,80,2048]{2,1,0:T(8,128)} %mul.43, bf16[8,80,2048]{2,1,0:T(8,128)(2,1)S(1)} %all-to-all-done.3), kind=kLoop, calls=%fused_computation.37 | loop fusion | flops 3768320 | bytes 8519680 | tf_op jit(solution)/shard_map/reduce_sum | solution.py:45
  218.2 3.5 %all-to-all-start.4 = ((bf16[4,20,2048]{2,1,0:T(8,128)(2,1)}), bf16[4,20,2048]{2,1,0:T(8,128)(2,1)S(1)}, u32[]{:S(2)}, u32[]{:S(2)}) async-start(bf16[4,20,2048]{2,1,0:T(8,128)(2,1)} %divide_convert_fusion), calls=%async_computation.4 | async-start | bytes 786432 | tf_op jit(solution)/shard_map/all_to_all | solution.py:100
  221.6 9.1 %all-to-all-done.4 = bf16[4,20,2048]{2,1,0:T(8,128)(2,1)S(1)} async-done(((bf16[4,20,2048]{2,1,0:T(8,128)(2,1)}), bf16[4,20,2048]{2,1,0:T(8,128)(2,1)S(1)}, u32[]{:S(2)}, u32[]{:S(2)}) %all-to-all-start.4) | async-done | bytes 327712 | tf_op jit(solution)/shard_map/all_to_all | solution.py:100
  (135 shorter events, 83.4 us)
Async XLA Ops:
  3.9 11.8 %all-to-all-start.1 = ((s32[4,1,20]{2,1,0:T(1,128)}), s32[4,1,20]{2,1,0:T(1,128)S(1)}, u32[]{:S(2)}, u32[]{:S(2)}) async-start(s32[4,1,20]{2,1,0:T(1,128)} %bitcast.7), calls=%async_computation.1 | async-start | bytes 4096 | tf_op jit(solution)/shard_map/all_to_all | solution.py:66
  15.7 15.1 %all-to-all-start = ((bf16[4,20,2048]{2,1,0:T(8,128)(2,1)}), bf16[4,20,2048]{2,1,0:T(8,128)(2,1)S(1)}, u32[]{:S(2)}, u32[]{:S(2)}) async-start(bf16[4,20,2048]{2,1,0:T(8,128)(2,1)} %reshape.229), calls=%async_computation | async-start | bytes 786432 | tf_op jit(solution)/shard_map/all_to_all | solution.py:63
  31.0 7.9 %copy-start = (bf16[1,2304,256]{2,1,0:T(8,128)(2,1)S(1)}, bf16[1,2304,256]{2,1,0:T(8,128)(2,1)}, u32[]{:S(2)}) copy-start(bf16[1,2304,256]{2,1,0:T(8,128)(2,1)} %param.10) | copy-start | bytes 3538948
  42.5 1.5 copy-start.1
  44.0 3.9 %collective-permute-start.1 = (s32[80]{0:T(128)S(1)}, s32[80]{0:T(128)S(1)}, u32[]{:S(2)}, u32[]{:S(2)}) collective-permute-start(s32[80]{0:T(128)S(1)} %get-tuple-element.327), channel_id=1, source_target_pairs={{28,0},{0,4},{4,8},{8,12},{12,16},{16,20},{20,24},{24,28},{29,1},{... | collective-permute-start | bytes 968 | tf_op jit(solution)/shard_map/while/body/eval_jaxpr/ppermute | solution.py:13
  44.0 7.4 %collective-permute-start = (bf16[80,16,128]{2,1,0:T(8,128)(2,1)S(1)}, bf16[80,16,128]{2,1,0:T(8,128)(2,1)S(1)}, u32[]{:S(2)}, u32[]{:S(2)}) collective-permute-start(bf16[80,16,128]{2,1,0:T(8,128)(2,1)S(1)} %get-tuple-element.326), channel_id=1, source_target_pairs={{28,0},{0,4},{4,8},{8,12},{12,16},{16,20},{20,24},{24,28},{29,1},{... | collective-permute-start | bytes 983048 | tf_op jit(solution)/shard_map/while/body/eval_jaxpr/ppermute | solution.py:13
  61.7 3.9 %collective-permute-start.1 = (s32[80]{0:T(128)S(1)}, s32[80]{0:T(128)S(1)}, u32[]{:S(2)}, u32[]{:S(2)}) collective-permute-start(s32[80]{0:T(128)S(1)} %get-tuple-element.327), channel_id=1, source_target_pairs={{28,0},{0,4},{4,8},{8,12},{12,16},{16,20},{20,24},{24,28},{29,1},{... | collective-permute-start | bytes 968 | tf_op jit(solution)/shard_map/while/body/eval_jaxpr/ppermute | solution.py:13
  61.8 7.5 %collective-permute-start = (bf16[80,16,128]{2,1,0:T(8,128)(2,1)S(1)}, bf16[80,16,128]{2,1,0:T(8,128)(2,1)S(1)}, u32[]{:S(2)}, u32[]{:S(2)}) collective-permute-start(bf16[80,16,128]{2,1,0:T(8,128)(2,1)S(1)} %get-tuple-element.326), channel_id=1, source_target_pairs={{28,0},{0,4},{4,8},{8,12},{12,16},{16,20},{20,24},{24,28},{29,1},{... | collective-permute-start | bytes 983048 | tf_op jit(solution)/shard_map/while/body/eval_jaxpr/ppermute | solution.py:13
  79.5 3.9 %collective-permute-start.1 = (s32[80]{0:T(128)S(1)}, s32[80]{0:T(128)S(1)}, u32[]{:S(2)}, u32[]{:S(2)}) collective-permute-start(s32[80]{0:T(128)S(1)} %get-tuple-element.327), channel_id=1, source_target_pairs={{28,0},{0,4},{4,8},{8,12},{12,16},{16,20},{20,24},{24,28},{29,1},{... | collective-permute-start | bytes 968 | tf_op jit(solution)/shard_map/while/body/eval_jaxpr/ppermute | solution.py:13
  79.6 7.5 %collective-permute-start = (bf16[80,16,128]{2,1,0:T(8,128)(2,1)S(1)}, bf16[80,16,128]{2,1,0:T(8,128)(2,1)S(1)}, u32[]{:S(2)}, u32[]{:S(2)}) collective-permute-start(bf16[80,16,128]{2,1,0:T(8,128)(2,1)S(1)} %get-tuple-element.326), channel_id=1, source_target_pairs={{28,0},{0,4},{4,8},{8,12},{12,16},{16,20},{20,24},{24,28},{29,1},{... | collective-permute-start | bytes 983048 | tf_op jit(solution)/shard_map/while/body/eval_jaxpr/ppermute | solution.py:13
  97.3 3.9 %collective-permute-start.1 = (s32[80]{0:T(128)S(1)}, s32[80]{0:T(128)S(1)}, u32[]{:S(2)}, u32[]{:S(2)}) collective-permute-start(s32[80]{0:T(128)S(1)} %get-tuple-element.327), channel_id=1, source_target_pairs={{28,0},{0,4},{4,8},{8,12},{12,16},{16,20},{20,24},{24,28},{29,1},{... | collective-permute-start | bytes 968 | tf_op jit(solution)/shard_map/while/body/eval_jaxpr/ppermute | solution.py:13
  97.4 7.5 %collective-permute-start = (bf16[80,16,128]{2,1,0:T(8,128)(2,1)S(1)}, bf16[80,16,128]{2,1,0:T(8,128)(2,1)S(1)}, u32[]{:S(2)}, u32[]{:S(2)}) collective-permute-start(bf16[80,16,128]{2,1,0:T(8,128)(2,1)S(1)} %get-tuple-element.326), channel_id=1, source_target_pairs={{28,0},{0,4},{4,8},{8,12},{12,16},{16,20},{20,24},{24,28},{29,1},{... | collective-permute-start | bytes 983048 | tf_op jit(solution)/shard_map/while/body/eval_jaxpr/ppermute | solution.py:13
  115.1 3.9 %collective-permute-start.1 = (s32[80]{0:T(128)S(1)}, s32[80]{0:T(128)S(1)}, u32[]{:S(2)}, u32[]{:S(2)}) collective-permute-start(s32[80]{0:T(128)S(1)} %get-tuple-element.327), channel_id=1, source_target_pairs={{28,0},{0,4},{4,8},{8,12},{12,16},{16,20},{20,24},{24,28},{29,1},{... | collective-permute-start | bytes 968 | tf_op jit(solution)/shard_map/while/body/eval_jaxpr/ppermute | solution.py:13
  115.2 7.5 %collective-permute-start = (bf16[80,16,128]{2,1,0:T(8,128)(2,1)S(1)}, bf16[80,16,128]{2,1,0:T(8,128)(2,1)S(1)}, u32[]{:S(2)}, u32[]{:S(2)}) collective-permute-start(bf16[80,16,128]{2,1,0:T(8,128)(2,1)S(1)} %get-tuple-element.326), channel_id=1, source_target_pairs={{28,0},{0,4},{4,8},{8,12},{12,16},{16,20},{20,24},{24,28},{29,1},{... | collective-permute-start | bytes 983048 | tf_op jit(solution)/shard_map/while/body/eval_jaxpr/ppermute | solution.py:13
  132.9 3.9 %collective-permute-start.1 = (s32[80]{0:T(128)S(1)}, s32[80]{0:T(128)S(1)}, u32[]{:S(2)}, u32[]{:S(2)}) collective-permute-start(s32[80]{0:T(128)S(1)} %get-tuple-element.327), channel_id=1, source_target_pairs={{28,0},{0,4},{4,8},{8,12},{12,16},{16,20},{20,24},{24,28},{29,1},{... | collective-permute-start | bytes 968 | tf_op jit(solution)/shard_map/while/body/eval_jaxpr/ppermute | solution.py:13
  133.0 7.5 %collective-permute-start = (bf16[80,16,128]{2,1,0:T(8,128)(2,1)S(1)}, bf16[80,16,128]{2,1,0:T(8,128)(2,1)S(1)}, u32[]{:S(2)}, u32[]{:S(2)}) collective-permute-start(bf16[80,16,128]{2,1,0:T(8,128)(2,1)S(1)} %get-tuple-element.326), channel_id=1, source_target_pairs={{28,0},{0,4},{4,8},{8,12},{12,16},{16,20},{20,24},{24,28},{29,1},{... | collective-permute-start | bytes 983048 | tf_op jit(solution)/shard_map/while/body/eval_jaxpr/ppermute | solution.py:13
  150.8 3.9 %collective-permute-start.1 = (s32[80]{0:T(128)S(1)}, s32[80]{0:T(128)S(1)}, u32[]{:S(2)}, u32[]{:S(2)}) collective-permute-start(s32[80]{0:T(128)S(1)} %get-tuple-element.327), channel_id=1, source_target_pairs={{28,0},{0,4},{4,8},{8,12},{12,16},{16,20},{20,24},{24,28},{29,1},{... | collective-permute-start | bytes 968 | tf_op jit(solution)/shard_map/while/body/eval_jaxpr/ppermute | solution.py:13
  150.8 7.5 %collective-permute-start = (bf16[80,16,128]{2,1,0:T(8,128)(2,1)S(1)}, bf16[80,16,128]{2,1,0:T(8,128)(2,1)S(1)}, u32[]{:S(2)}, u32[]{:S(2)}) collective-permute-start(bf16[80,16,128]{2,1,0:T(8,128)(2,1)S(1)} %get-tuple-element.326), channel_id=1, source_target_pairs={{28,0},{0,4},{4,8},{8,12},{12,16},{16,20},{20,24},{24,28},{29,1},{... | collective-permute-start | bytes 983048 | tf_op jit(solution)/shard_map/while/body/eval_jaxpr/ppermute | solution.py:13
  176.2 35.8 %all-to-all-start.3 = ((bf16[8,80,2048]{2,1,0:T(8,128)(2,1)}), bf16[8,80,2048]{2,1,0:T(8,128)(2,1)S(1)}, u32[]{:S(2)}, u32[]{:S(2)}) async-start(bf16[8,80,2048]{2,1,0:T(8,128)(2,1)} %get-tuple-element.228), calls=%async_computation.3 | async-start | bytes 5242880 | tf_op jit(solution)/shard_map/all_to_all | solution.py:94
  218.2 12.5 %all-to-all-start.4 = ((bf16[4,20,2048]{2,1,0:T(8,128)(2,1)}), bf16[4,20,2048]{2,1,0:T(8,128)(2,1)S(1)}, u32[]{:S(2)}, u32[]{:S(2)}) async-start(bf16[4,20,2048]{2,1,0:T(8,128)(2,1)} %divide_convert_fusion), calls=%async_computation.4 | async-start | bytes 786432 | tf_op jit(solution)/shard_map/all_to_all | solution.py:100
where the time goes:
time: 234 us; the launch traced here: 232 us
  waiting for transfers between devices  82.1 us (35%)
  other arithmetic  46.1 us (20%)
  matrix products  45.3 us (19%)
  local copies, waits for them, and re-layouts  30 us (13%)
  starting transfers between devices  20.3 us (9%)
  blocking collectives  7.47 us (3%)
    ppermute x14, waiting for transfers between devices, shifted(): return lax.ppermute(block, axis, route)  42.9 us
    reduce_sum x8, other arithmetic, shard_partial(): total = jnp.sum(weights, axis=-1)  30.7 us
    dot_general x8, matrix products, shard_partial(): jnp.einsum('shk,kd->shd', weights.astype(jnp.bfloat16), values, preferred...  23.8 us
    dot_general x8, matrix products, shard_partial(): jnp.einsum('shd,kd->shk', query, keys, preferred_element_type=jnp.float32)  21.5 us
    all_to_all x1, waiting for transfers between devices, per_device(): lax.all_to_all(final[2], 'ctx', split_axis=0, concat_axis=0, tiled=True)  19.4 us
    mul x2, local copies, waits for them, and re-layouts, merge_parts(): share[..., None] * widened  10.3 us
    all_to_all x1, waiting for transfers between devices, per_device(): lax.all_to_all(send_q.reshape(groups, capacity, H * HD), 'req', split_axi...  9.66 us
    all_to_all x1, waiting for transfers between devices, per_device(): lax.all_to_all(output, 'req', split_axis=0, concat_axis=0, tiled=True)  9.05 us
  transfers between devices with their start and end apart: 18, of which 18 were waited for; matrix products, arithmetic and copies ran while one was open for 11% of the time, Pallas kernels for 0%

commit v1 on v0

v1 whole, which is shorter than its diff:
```python
import functools
import math

import jax
import jax.numpy as jnp
from jax import lax
from jax.experimental import pallas as pl
from jax.experimental.pallas import tpu as pltpu
from jax.sharding import PartitionSpec as P

H = 16
HD = 128
WIDE = H * HD
META = 128
BALANCE = True
LOW = -1e30
SCALE = HD**-0.5
EXP_SCALE = SCALE * math.log2(math.e)
NT = (((1,), (1,)), ((), ()))
NN = (((1,), (0,)), ((), ()))
VMEM = pl.BlockSpec(memory_space=pltpu.VMEM)
SMEM = pl.BlockSpec(memory_space=pltpu.SMEM)


def dot(a, b, dims=NN):
    return lax.dot_general(a, b, dims, preferred_element_type=jnp.float32)


def iota(shape, dim):
    return lax.broadcasted_iota(jnp.int32, shape, dim)


def row_of(column):
    return jnp.transpose(jnp.broadcast_to(column, (column.shape[0], 128)), (1, 0))[:1, :]


def call(body, out_shape, in_specs, name, scratch=(), limit=32, cost=None):
    many = isinstance(out_shape, list)
    return pl.pallas_call(
        body,
        out_shape=out_shape,
        in_specs=in_specs,
        out_specs=[VMEM] * len(out_shape) if many else VMEM,
        scratch_shapes=list(scratch),
        compiler_params=pltpu.CompilerParams(vmem_limit_bytes=limit << 20),
        cost_estimate=cost,
        name=name,
    )


def route_kernel(block, me_ref, req_ref, pos_ref, q_ref, *outs):
    sends, back_ref = outs[:-1], outs[-1]
    rows = q_ref.shape[0]
    target_c = req_ref[...]
    target_r = row_of(target_c.astype(jnp.float32)).astype(jnp.int32)
    earlier_c = (target_c == target_r) & (iota((rows, rows), 1) < iota((rows, rows), 0))
    earlier_r = (target_c == target_r) & (iota((rows, rows), 0) < iota((rows, rows), 1))
    rank_c = jnp.sum(earlier_c.astype(jnp.int32), axis=1, keepdims=True)
    rank_r = jnp.sum(earlier_r.astype(jnp.int32), axis=0, keepdims=True)
    slot_c = (target_c ^ me_ref[1]) * block + rank_c
    slot_r = (target_r ^ me_ref[1]) * block + rank_r
    total = len(sends) * block
    back_ref[...] = (slot_c == iota((rows, total), 1)).astype(jnp.bfloat16)
    place = (slot_r == iota((total, rows), 0)).astype(jnp.bfloat16)
    plus = pos_ref[...] + 1
    place_f = place.astype(jnp.float32)
    high = jnp.sum(place_f * (plus >> 8).astype(jnp.float32), axis=1, keepdims=True)
    low = jnp.sum(place_f * (plus & 255).astype(jnp.float32), axis=1, keepdims=True)
    lane = iota((total, META), 1)
    meta = jnp.where(lane == 0, high, jnp.where(lane == 1, low, 0.0)).astype(jnp.bfloat16)
    moved = dot(place, q_ref[...]).astype(jnp.bfloat16)
    for d, out in enumerate(sends):
        out[:, :WIDE] = moved[d * block : (d + 1) * block]
        out[:, WIDE:] = meta[d * block : (d + 1) * block]


def sort_kernel(*refs):
    blocks, out, back_ref = refs[:-2], refs[-2], refs[-1]
    slots = out.shape[0]
    joined = jnp.concatenate([b[...] for b in blocks], axis=0)
    total = joined.shape[0]
    meta = joined[:, WIDE:].astype(jnp.float32)
    pos_c = meta[:, 0:1] * 256.0 + meta[:, 1:2]
    pos_r = row_of(pos_c)
    i0, i1 = iota((total, total), 0), iota((total, total), 1)
    ahead_r = (pos_c > pos_r) | ((pos_c == pos_r) & (i0 < i1))
    ahead_c = (pos_r > pos_c) | ((pos_r == pos_c) & (i1 < i0))
    rank_r = jnp.sum(ahead_r.astype(jnp.int32), axis=0, keepdims=True)
    rank_c = jnp.sum(ahead_c.astype(jnp.int32), axis=1, keepdims=True)
    place = (rank_r == iota((slots, total), 0)).astype(jnp.bfloat16)
    back_ref[...] = (rank_c == iota((total, slots), 1)).astype(jnp.bfloat16)
    out[...] = dot(place, joined).astype(jnp.bfloat16)


def keys_kernel(*refs):
    pieces, k_ref, vt_ref = refs[:-2], refs[-2], refs[-1]
    piece = pieces[0].shape[0]
    for i, ref in enumerate(pieces):
        k_ref[i * piece : (i + 1) * piece, :] = ref[:, :HD]
        vt_ref[:HD, i * piece : (i + 1) * piece] = jnp.transpose(ref[:, HD:], (1, 0))
    extra = vt_ref.shape[0] - HD
    ones = (iota((extra, vt_ref.shape[1]), 0) == 0).astype(jnp.bfloat16)
    vt_ref[HD:, :] = ones


def flash_kernel(pieces, piece, step, info_ref, len_ref, pq_ref, k_ref, vt_ref, out_ref, acc_ref, q_ref):
    length = len_ref[info_ref[2 * pieces]]
    slots = pq_ref.shape[0]

    def tile(first, count):
        width = count * H
        rows = pl.ds(first, count)
        meta = pq_ref[rows, WIDE:].astype(jnp.float32)
        pos = meta[:, 0:1] * 256.0 + meta[:, 1:2] - 1.0
        last = jnp.minimum(pos, (length - 1).astype(jnp.float32))
        top_last = jnp.max(last).astype(jnp.int32)
        last_r = jnp.concatenate([row_of(last)] * H, axis=1).astype(jnp.int32)
        live = jnp.int32(0)
        for b in range(pieces):
            live += (info_ref[b] <= top_last).astype(jnp.int32)
        for h in range(H):
            q_ref[h * count : (h + 1) * count, :] = pq_ref[rows, h * HD : (h + 1) * HD]
        acc_ref[:, :width] = jnp.zeros((acc_ref.shape[0], width), jnp.float32)

        def body(b, top):
            base = info_ref[pieces + b] * piece
            start = info_ref[b]

            def scores(g):
                keys = pl.ds(pl.multiple_of(base + g * step, step), step)
                return dot(k_ref[keys, :], q_ref[:width, :], NT)

            s = scores(0)
            for g in range(piece // step):
                later = scores(g + 1) if (g + 1) * step < piece else None
                s = jnp.where(iota((step, width), 0) <= last_r - (start + g * step), s, LOW)
                new = jnp.maximum(top, jnp.max(s, axis=0, keepdims=True))
                weights = jnp.exp2((s - new) * EXP_SCALE).astype(jnp.bfloat16)
                keys = pl.ds(pl.multiple_of(base + g * step, step), step)
                acc_ref[:, :width] = acc_ref[:, :width] * jnp.exp2((top - new) * EXP_SCALE) + dot(
                    vt_ref[:, keys], weights
                )
                top, s = new, later
            return top

        top = lax.fori_loop(0, live, body, jnp.full((1, width), 0.1 * LOW, jnp.float32))
        total = acc_ref[HD : HD + 1, :width]
        some = total > 0.0
        safe = jnp.where(some, total, 1.0)
        part = jnp.transpose(acc_ref[:HD, :width] / safe, (1, 0))
        lse = jnp.where(some, top * SCALE + jnp.log(safe), LOW)
        lse = jnp.transpose(jnp.broadcast_to(lse, (128, width)), (1, 0))
        lane = iota((count, META), 1)
        packed = jnp.zeros((count, META), jnp.float32)
        for h in range(H):
            out_ref[rows, h * HD : (h + 1) * HD] = part[h * count : (h + 1) * count].astype(jnp.bfloat16)
            packed = jnp.where(lane % H == h, lse[h * count : (h + 1) * count], packed)
        a = packed.astype(jnp.bfloat16).astype(jnp.float32)
        b = (packed - a).astype(jnp.bfloat16).astype(jnp.float32)
        c = packed - a - b
        packed = jnp.where(lane < H, a, jnp.where(lane < 2 * H, b, jnp.where(lane < 3 * H, c, 0.0)))
        out_ref[rows, WIDE:] = packed.astype(jnp.bfloat16)

    big = 32

    def one(j, carry):
        tile(pl.multiple_of(j * big, big), big)
        return carry

    lax.fori_loop(0, slots // big, one, 0)
    if slots % big:
        tile(slots // big * big, slots % big)


def merge_kernel(count, *refs):
    parts, back_ref, outs = refs[:count], refs[count], refs[count + 1 :]
    lses = []
    for part in parts:
        meta = part[:, WIDE:].astype(jnp.float32)
        lses.append(meta[:, :H] + meta[:, H : 2 * H] + meta[:, 2 * H : 3 * H])
    high = functools.reduce(jnp.maximum, lses)
    shares = [jnp.exp(lse - high) for lse in lses]
    total = functools.reduce(jnp.add, shares)
    shares = [share / total for share in shares]
    block = outs[0].shape[0]
    for h in range(H):
        cols = slice(h * HD, (h + 1) * HD)
        merged = sum(s[:, h : h + 1] * p[:, cols].astype(jnp.float32) for s, p in zip(shares, parts))
        placed = dot(back_ref[...], merged.astype(jnp.bfloat16)).astype(jnp.bfloat16)
        for d, out in enumerate(outs):
            out[:, cols] = placed[d * block : (d + 1) * block]


def unroute_kernel(*refs):
    blocks, back_ref, out = refs[:-2], refs[-2], refs[-1]
    joined = jnp.concatenate([b[...] for b in blocks], axis=0)
    out[...] = dot(back_ref[...], joined).astype(jnp.bfloat16)


def swapped(block, axis, distance):
    devices = range(lax.axis_size(axis))
    return lax.ppermute(block, axis, [(i, i ^ distance) for i in devices])


def per_device(queries, q_pos, req_of, cache, cache_len):
    tok_rows = queries.shape[0]
    groups = lax.axis_size("req")
    cycle = lax.axis_size("ctx")
    chips = cycle // 2
    capacity = 5 * tok_rows // (4 * groups)
    slots = groups * capacity
    block = -(-capacity // 8) * 8
    wide = WIDE + META
    shard_len = cache.shape[1]
    half = shard_len // 2
    here = lax.axis_index("ctx")
    mine = lax.axis_index("req")
    me = jnp.stack([here, mine]).astype(jnp.int32)
    bf = lambda *shape: jax.ShapeDtypeStruct(shape, jnp.bfloat16)

    *sends, back_tok = call(
        functools.partial(route_kernel, block),
        [bf(block, wide)] * groups + [bf(tok_rows, groups * block)],
        [SMEM] + [VMEM] * 3,
        "route",
    )(me, req_of, q_pos.reshape(1, tok_rows), queries)
    blocks = [sends[0]] + [swapped(sends[d], "req", d) for d in range(1, groups)]

    span = cache[0]
    other = cycle - 2
    kept, away = span[:half], span[half:]
    chip = here // 2
    if BALANCE:
        away = swapped(away, "ctx", other)
        partner = here ^ other
    else:
        partner = here
    kept_sib, away_sib = swapped(kept, "ctx", 1), swapped(away, "ctx", 1)
    pieces = [kept, kept_sib, away, away_sib]
    starts = jnp.stack(
        [here * shard_len, (here ^ 1) * shard_len, partner * shard_len + half, (partner ^ 1) * shard_len + half]
    ).astype(jnp.int32)
    order = jnp.sum(starts[None, :] < starts[:, None], axis=1)
    onehot = order[None, :] == jnp.arange(4)[:, None]
    info = jnp.concatenate(
        [
            jnp.sum(jnp.where(onehot, starts[None, :], 0), axis=1),
            jnp.sum(jnp.where(onehot, jnp.arange(4)[None, :], 0), axis=1),
            mine[None],
        ]
    ).astype(jnp.int32)
    keys = 4 * half
    k_all, vt_all = call(keys_kernel, [bf(keys, HD), bf(HD + 16, keys)], [VMEM] * 4, "keys")(*pieces)

    sorted_q, back_slot = call(
        sort_kernel, [bf(slots, wide), bf(groups * block, slots)], [VMEM] * groups, "sort"
    )(*blocks)
    visiting = [sorted_q] + [swapped(sorted_q, "ctx", 2 * d) for d in range(1, chips)]

    flash = call(
        functools.partial(flash_kernel, 4, half, 384),
        bf(slots, wide),
        [SMEM, SMEM] + [VMEM] * 3,
        "flash",
        scratch=[pltpu.VMEM((HD + 16, 512), jnp.float32), pltpu.VMEM((512, HD), jnp.bfloat16)],
        limit=48,
        cost=pl.CostEstimate(
            flops=4 * slots * H * keys * HD, bytes_accessed=keys * 512, transcendentals=slots * H * keys
        ),
    )
    parts = [flash(info, cache_len, q, k_all, vt_all) for q in visiting]
    home = [parts[0]] + [swapped(parts[d], "ctx", 2 * d) for d in range(1, chips)]
    outs = call(
        functools.partial(merge_kernel, chips), [bf(block, WIDE)] * groups, [VMEM] * (chips + 1), "merge"
    )(*home, back_slot)
    back = [outs[0]] + [swapped(outs[d], "req", d) for d in range(1, groups)]
    return call(unroute_kernel, bf(tok_rows, WIDE), [VMEM] * (groups + 1), "unroute")(*back, back_tok)


def solution(mesh):
    in_specs = (
        P(("ctx", "req"), None),
        P(("ctx", "req")),
        P(("ctx", "req"), None),
        P("req", "ctx", None),
        P(),
    )
    out_specs = P(("ctx", "req"), None)
    return jax.shard_map(
        per_device, mesh=mesh, in_specs=in_specs, out_specs=out_specs, check_vma=False
    )
```

time: 234 us -> 100 us (0.43)
  waiting for transfers between devices: 82.1 us -> 32.1 us
  other arithmetic: 46.1 us -> 0.56 us
  matrix products: 45.3 us -> 0 us
  Pallas kernels: 0 us -> 44.8 us
  local copies, waits for them, and re-layouts: 30 us -> 1.47 us
  blocking collectives: 7.47 us -> 0 us
    dot_general x16 -> x0, matrix products: 45.3 us -> none  [the longest x8 23.8 us: shard_partial(): jnp.einsum('shk,kd->shd', weights.astype(jnp.bfloat16), values, preferred...]
    pallas_call x0 -> x9, Pallas kernels: none -> 44.8 us  [the longest x4 40.8 us: per_device(): parts = [flash(info, cache_len, q, k_all, vt_all) for q in visiting]]
    all_to_all x4 -> x0, waiting for transfers between devices: 39.2 us -> none  [the longest x1 19.4 us: per_device(): lax.all_to_all(final[2], 'ctx', split_axis=0, concat_axis=0, tiled=True)]
    reduce_sum x11 -> x2, other arithmetic: 35.7 us -> 0.33 us  [the longest x1 0.18 us: per_device(): order = jnp.sum(starts[None, :] < starts[:, None], axis=1)]
    ppermute x14 -> x15, starting transfers between devices: 2.95 us -> 21 us  [swapped(): return lax.ppermute(block, axis, [(i, i ^ distance) for i in devices])]
    all_to_all x4 -> x0, starting transfers between devices: 17.4 us -> none  [the longest x1 6.32 us: per_device(): lax.all_to_all(send_pos.reshape(groups, capacity), 'req', split_axis=0, c...]
    ppermute x14 -> x15, waiting for transfers between devices: 42.9 us -> 32.1 us  [swapped(): return lax.ppermute(block, axis, [(i, i ^ distance) for i in devices])]
    mul x2 -> x0, local copies, waits for them, and re-layouts: 10.3 us -> none  [merge_parts(): share[..., None] * widened]
  transfers between devices with their start and end apart: 18 -> 15, of which waited for: 18 -> 7; matrix products, arithmetic and copies ran while one was open for 11% -> 1% of each run, Pallas kernels for 0% -> 43%
where the time goes in v1:
time: 100 us
  Pallas kernels  44.8 us (45%)
  waiting for transfers between devices  32.1 us (32%)
  starting transfers between devices  21 us (21%)
  local copies, waits for them, and re-layouts  1.47 us (1%)
    pallas_call x4, Pallas kernels, per_device(): parts = [flash(info, cache_len, q, k_all, vt_all) for q in visiting]  40.8 us
    ppermute x15, waiting for transfers between devices, swapped(): return lax.ppermute(block, axis, [(i, i ^ distance) for i in devices])  32.1 us
    ppermute x15, starting transfers between devices, swapped(): return lax.ppermute(block, axis, [(i, i ^ distance) for i in devices])  21 us
  transfers between devices with their start and end apart: 15, of which 7 were waited for; matrix products, arithmetic and copies ran while one was open for 1% of the time, Pallas kernels for 43%

profile of v1, /device:TPU:0, one launch (start us, length us, event | category | flops | bytes accessed | tf_op | source)
XLA Modules:
  0.0 100.1 jit_solution(13312950738016461153)
XLA Ops:
  0.0 1.4 %slice_bitcast_fusion = (bf16[1152,256]{1,0:T(8,128)(2,1)S(1)}, bf16[1152,256]{1,0:T(8,128)(2,1)S(1)}) fusion(bf16[1,2304,256]{2,1,0:T(8,128)(2,1)} %param.8), kind=kLoop, calls=%fused_computation | loop fusion | bytes 2359296 | tf_op jit(solution)/shard_map/slice | solution.py:231
  1.4 4.0 %collective-permute-start.4 = (bf16[1152,256]{1,0:T(8,128)(2,1)S(1)}, bf16[1152,256]{1,0:T(8,128)(2,1)S(1)}, u32[]{:S(2)}, u32[]{:S(2)}) collective-permute-start(bf16[1152,256]{1,0:T(8,128)(2,1)S(1)} %get-tuple-element.33), channel_id=1, source_target_pairs={{0,24},{4,28},{8,16},{12,20},{16,8},{20,12},{24,0},{28,4},{1,25},{... | collective-permute-start | bytes 1769480 | tf_op jit(solution)/shard_map/ppermute | solution.py:202
  5.3 13.3 %collective-permute-done.4.refs_2_ = bf16[1152,256]{1,0:T(8,128)(2,1)S(1)} collective-permute-done((bf16[1152,256]{1,0:T(8,128)(2,1)S(1)}, bf16[1152,256]{1,0:T(8,128)(2,1)S(1)}, u32[]{:S(2)}, u32[]{:S(2)}) %collective-permute-start.4) | collective-permute-done | bytes 589856 | tf_op jit(solution)/shard_map/ppermute | solution.py:202
  18.7 0.1 copy.7.req_ref
  18.9 0.9 route.1
  19.8 1.8 %collective-permute-start = (bf16[24,2176]{1,0:T(8,128)(2,1)S(1)}, bf16[24,2176]{1,0:T(8,128)(2,1)S(1)}, u32[]{:S(2)}, u32[]{:S(2)}) collective-permute-start(bf16[24,2176]{1,0:T(8,128)(2,1)S(1)} %get-tuple-element.19), channel_id=1, source_target_pairs={{0,1},{1,0},{2,3},{3,2},{4,5},{5,4},{6,7},{7,6},{8,9},{9,8},{10,11... | collective-permute-start | bytes 313352 | tf_op jit(solution)/shard_map/ppermute | solution.py:202
  21.6 2.6 %collective-permute-start.1 = (bf16[24,2176]{1,0:T(8,128)(2,1)S(1)}, bf16[24,2176]{1,0:T(8,128)(2,1)S(1)}, u32[]{:S(2)}, u32[]{:S(2)}) collective-permute-start(bf16[24,2176]{1,0:T(8,128)(2,1)S(1)} %get-tuple-element.20), channel_id=1, source_target_pairs={{0,2},{1,3},{2,0},{3,1},{4,6},{5,7},{6,4},{7,5},{8,10},{9,11},{10,... | collective-permute-start | bytes 313352 | tf_op jit(solution)/shard_map/ppermute | solution.py:202
  24.3 1.0 collective-permute-done.refs_1_
  25.2 7.5 %collective-permute-done.1.refs_2_ = bf16[24,2176]{1,0:T(8,128)(2,1)S(1)} collective-permute-done((bf16[24,2176]{1,0:T(8,128)(2,1)S(1)}, bf16[24,2176]{1,0:T(8,128)(2,1)S(1)}, u32[]{:S(2)}, u32[]{:S(2)}) %collective-permute-start.1) | collective-permute-done | bytes 104480 | tf_op jit(solution)/shard_map/ppermute | solution.py:202
  32.8 0.5 sort.1
  33.3 1.6 %collective-permute-start.6 = (bf16[80,2176]{1,0:T(8,128)(2,1)S(1)}, bf16[80,2176]{1,0:T(8,128)(2,1)S(1)}, u32[]{:S(2)}, u32[]{:S(2)}) collective-permute-start(bf16[80,2176]{1,0:T(8,128)(2,1)S(1)} %get-tuple-element.22.pq_ref), channel_id=1, source_target_pairs={{0,8},{4,12},{8,0},{12,4},{16,24},{20,28},{24,16},{28,20},{1,9},{5... | collective-permute-start | bytes 1044488 | tf_op jit(solution)/shard_map/ppermute | solution.py:202
  34.8 0.1 pad_add_fusion
  34.9 0.2 convert_reduce_fusion
  35.1 0.1 select_reduce_fusion.1
  35.2 1.6 %collective-permute-start.8 = (bf16[80,2176]{1,0:T(8,128)(2,1)S(1)}, bf16[80,2176]{1,0:T(8,128)(2,1)S(1)}, u32[]{:S(2)}, u32[]{:S(2)}) collective-permute-start(bf16[80,2176]{1,0:T(8,128)(2,1)S(1)} %get-tuple-element.22.pq_ref), channel_id=1, source_target_pairs={{0,16},{4,20},{8,24},{12,28},{16,0},{20,4},{24,8},{28,12},{1,17},{... | collective-permute-start | bytes 1044488 | tf_op jit(solution)/shard_map/ppermute | solution.py:202
  36.8 0.1 pad_add_fusion.1.info_ref
  36.9 0.5 collective-permute-start.10
  37.4 0.5 keys.1
  37.9 6.5 %collective-permute-done.6.pq_ref = bf16[80,2176]{1,0:T(8,128)(2,1)S(1)} collective-permute-done((bf16[80,2176]{1,0:T(8,128)(2,1)S(1)}, bf16[80,2176]{1,0:T(8,128)(2,1)S(1)}, u32[]{:S(2)}, u32[]{:S(2)}) %collective-permute-start.6) | collective-permute-done | bytes 348192 | tf_op jit(solution)/shard_map/ppermute | solution.py:202
  44.4 10.2 %flash.5 = bf16[80,2176]{1,0:T(8,128)(2,1)S(1)} custom-call(s32[9]{0:T(128)S(1)} %pad_add_fusion.1.info_ref, s32[4]{0:T(128)S(1)} %copy-done.2, bf16[80,2176]{1,0:T(8,128)(2,1)S(1)} %collective-permute-done.6.pq_ref, bf16[4608,128]{1,0:T(8,128)(2,1)S(1)} %get-tuple-element.23.k_ref, bf16[144,4608]{1,0:T(8,128)(2,1)S(1)} %get-tuple-element.24.vt_ref), custom_call_target="tpu_custom_call" | custom-call | flops 3019898880 | bytes 2359296 | tf_op jit(solution)/shard_map/flash/pallas_call | solution.py:271
  54.6 1.3 %collective-permute-start.7 = (bf16[80,2176]{1,0:T(8,128)(2,1)S(1)}, bf16[80,2176]{1,0:T(8,128)(2,1)S(1)}, u32[]{:S(2)}, u32[]{:S(2)}) collective-permute-start(bf16[80,2176]{1,0:T(8,128)(2,1)S(1)} %flash.5), channel_id=1, source_target_pairs={{0,8},{4,12},{8,0},{12,4},{16,24},{20,28},{24,16},{28,20},{1,9},{5... | collective-permute-start | bytes 1044488 | tf_op jit(solution)/shard_map/ppermute | solution.py:202
  55.9 10.2 %flash.6 = bf16[80,2176]{1,0:T(8,128)(2,1)S(1)} custom-call(s32[9]{0:T(128)S(1)} %pad_add_fusion.1.info_ref, s32[4]{0:T(128)S(1)} %copy-done.2, bf16[80,2176]{1,0:T(8,128)(2,1)S(1)} %collective-permute-done.8.pq_ref, bf16[4608,128]{1,0:T(8,128)(2,1)S(1)} %get-tuple-element.23.k_ref, bf16[144,4608]{1,0:T(8,128)(2,1)S(1)} %get-tuple-element.24.vt_ref), custom_call_target="tpu_custom_call" | custom-call | flops 3019898880 | bytes 2359296 | tf_op jit(solution)/shard_map/flash/pallas_call | solution.py:271
  66.1 0.9 collective-permute-start.9
  67.1 10.2 %flash.7 = bf16[80,2176]{1,0:T(8,128)(2,1)S(1)} custom-call(s32[9]{0:T(128)S(1)} %pad_add_fusion.1.info_ref, s32[4]{0:T(128)S(1)} %copy-done.2, bf16[80,2176]{1,0:T(8,128)(2,1)S(1)} %collective-permute-done.10.pq_ref, bf16[4608,128]{1,0:T(8,128)(2,1)S(1)} %get-tuple-element.23.k_ref, bf16[144,4608]{1,0:T(8,128)(2,1)S(1)} %get-tuple-element.24.vt_ref), custom_call_target="tpu_custom_call" | custom-call | flops 3019898880 | bytes 2359296 | tf_op jit(solution)/shard_map/flash/pallas_call | solution.py:271
  77.3 2.3 %collective-permute-start.11 = (bf16[80,2176]{1,0:T(8,128)(2,1)S(1)}, bf16[80,2176]{1,0:T(8,128)(2,1)S(1)}, u32[]{:S(2)}, u32[]{:S(2)}) collective-permute-start(bf16[80,2176]{1,0:T(8,128)(2,1)S(1)} %flash.7), channel_id=1, source_target_pairs={{0,24},{4,28},{8,16},{12,20},{16,8},{20,12},{24,0},{28,4},{1,25},{... | collective-permute-start | bytes 1044488 | tf_op jit(solution)/shard_map/ppermute | solution.py:202
  79.5 10.2 %flash.4.refs_0_ = bf16[80,2176]{1,0:T(8,128)(2,1)S(1)} custom-call(s32[9]{0:T(128)S(1)} %pad_add_fusion.1.info_ref, s32[4]{0:T(128)S(1)} %copy-done.2, bf16[80,2176]{1,0:T(8,128)(2,1)S(1)} %get-tuple-element.22.pq_ref, bf16[4608,128]{1,0:T(8,128)(2,1)S(1)} %get-tuple-element.23.k_ref, bf16[144,4608]{1,0:T(8,128)(2,1)S(1)} %get-tuple-element.24.vt_ref), custom_call_target="tpu_custom_call" | custom-call | flops 3019898880 | bytes 2359296 | tf_op jit(solution)/shard_map/flash/pallas_call | solution.py:271
  89.8 1.2 %merge.1 = (bf16[24,2048]{1,0:T(8,128)(2,1)S(1)}, bf16[24,2048]{1,0:T(8,128)(2,1)S(1)}, bf16[24,2048]{1,0:T(8,128)(2,1)S(1)}, bf16[24,2048]{1,0:T(8,128)(2,1)S(1)}) custom-call(bf16[80,2176]{1,0:T(8,128)(2,1)S(1)} %flash.4.refs_0_, bf16[80,2176]{1,0:T(8,128)(2,1)S(1)} %collective-permute-done.7.refs_1_, bf16[80,2176]{1,0:T(8,128)(2,1)S(1)} %collective-permute-done.9.refs_2_, ...), custom_call_target="tpu_custom_call" | custom-call | tf_op jit(solution)/shard_map/merge/pallas_call | solution.py:273
  91.1 4.3 %collective-permute-start.14 = (bf16[24,2048]{1,0:T(8,128)(2,1)S(1)}, bf16[24,2048]{1,0:T(8,128)(2,1)S(1)}, u32[]{:S(2)}, u32[]{:S(2)}) collective-permute-start(bf16[24,2048]{1,0:T(8,128)(2,1)S(1)} %get-tuple-element.29), channel_id=1, source_target_pairs={{0,3},{1,2},{2,1},{3,0},{4,7},{5,6},{6,5},{7,4},{8,11},{9,10},{10,... | collective-permute-start | bytes 294920 | tf_op jit(solution)/shard_map/ppermute | solution.py:202
  95.4 0.2 collective-permute-done.12.refs_1_
  95.6 1.0 %collective-permute-done.13.refs_2_ = bf16[24,2048]{1,0:T(8,128)(2,1)S(1)} collective-permute-done((bf16[24,2048]{1,0:T(8,128)(2,1)S(1)}, bf16[24,2048]{1,0:T(8,128)(2,1)S(1)}, u32[]{:S(2)}, u32[]{:S(2)}) %collective-permute-start.13) | collective-permute-done | bytes 98336 | tf_op jit(solution)/shard_map/ppermute | solution.py:202
  96.7 2.5 %collective-permute-done.14.refs_3_ = bf16[24,2048]{1,0:T(8,128)(2,1)S(1)} collective-permute-done((bf16[24,2048]{1,0:T(8,128)(2,1)S(1)}, bf16[24,2048]{1,0:T(8,128)(2,1)S(1)}, u32[]{:S(2)}, u32[]{:S(2)}) %collective-permute-start.14) | collective-permute-done | bytes 98336 | tf_op jit(solution)/shard_map/ppermute | solution.py:202
  99.1 0.9 unroute.1
  (22 shorter events, 0.3 us)
Async XLA Ops:
  0.0 18.7 %copy-start.3 = (s32[64,1]{0,1:T(1,128)S(1)}, s32[64,1]{0,1:T(1,128)}, u32[]{:S(2)}) copy-start(s32[64,1]{0,1:T(1,128)} %param.7) | copy-start | bytes 772
  0.0 18.8 %copy-start.1 = (s32[64]{0:T(128)S(1)}, s32[64]{0:T(128)}, u32[]{:S(2)}) copy-start(s32[64]{0:T(128)} %param.6) | copy-start | bytes 772
  0.0 18.8 %copy-start = (bf16[64,2048]{1,0:T(8,128)(2,1)S(1)}, bf16[64,2048]{1,0:T(8,128)(2,1)}, u32[]{:S(2)}) copy-start(bf16[64,2048]{1,0:T(8,128)(2,1)} %q_ref.1) | copy-start | bytes 786436
  1.4 17.3 %collective-permute-start.4 = (bf16[1152,256]{1,0:T(8,128)(2,1)S(1)}, bf16[1152,256]{1,0:T(8,128)(2,1)S(1)}, u32[]{:S(2)}, u32[]{:S(2)}) collective-permute-start(bf16[1152,256]{1,0:T(8,128)(2,1)S(1)} %get-tuple-element.33), channel_id=1, source_target_pairs={{0,24},{4,28},{8,16},{12,20},{16,8},{20,12},{24,0},{28,4},{1,25},{... | collective-permute-start | bytes 1769480 | tf_op jit(solution)/shard_map/ppermute | solution.py:202
  5.3 32.0 %collective-permute-start.3 = (bf16[1152,256]{1,0:T(8,128)(2,1)S(1)}, bf16[1152,256]{1,0:T(8,128)(2,1)S(1)}, u32[]{:S(2)}, u32[]{:S(2)}) collective-permute-start(bf16[1152,256]{1,0:T(8,128)(2,1)S(1)} %get-tuple-element.34.refs_0_), channel_id=1, source_target_pairs={{0,4},{4,0},{8,12},{12,8},{16,20},{20,16},{24,28},{28,24},{1,5},{5... | collective-permute-start | bytes 1769480 | tf_op jit(solution)/shard_map/ppermute | solution.py:202
  18.7 18.7 %collective-permute-start.5 = (bf16[1152,256]{1,0:T(8,128)(2,1)S(1)}, bf16[1152,256]{1,0:T(8,128)(2,1)S(1)}, u32[]{:S(2)}, u32[]{:S(2)}) collective-permute-start(bf16[1152,256]{1,0:T(8,128)(2,1)S(1)} %collective-permute-done.4.refs_2_), channel_id=1, source_target_pairs={{0,4},{4,0},{8,12},{12,8},{16,20},{20,16},{24,28},{28,24},{1,5},{5... | collective-permute-start | bytes 1769480 | tf_op jit(solution)/shard_map/ppermute | solution.py:202
  19.8 5.4 %collective-permute-start = (bf16[24,2176]{1,0:T(8,128)(2,1)S(1)}, bf16[24,2176]{1,0:T(8,128)(2,1)S(1)}, u32[]{:S(2)}, u32[]{:S(2)}) collective-permute-start(bf16[24,2176]{1,0:T(8,128)(2,1)S(1)} %get-tuple-element.19), channel_id=1, source_target_pairs={{0,1},{1,0},{2,3},{3,2},{4,5},{5,4},{6,7},{7,6},{8,9},{9,8},{10,11... | collective-permute-start | bytes 313352 | tf_op jit(solution)/shard_map/ppermute | solution.py:202
  21.6 11.1 %collective-permute-start.1 = (bf16[24,2176]{1,0:T(8,128)(2,1)S(1)}, bf16[24,2176]{1,0:T(8,128)(2,1)S(1)}, u32[]{:S(2)}, u32[]{:S(2)}) collective-permute-start(bf16[24,2176]{1,0:T(8,128)(2,1)S(1)} %get-tuple-element.20), channel_id=1, source_target_pairs={{0,2},{1,3},{2,0},{3,1},{4,6},{5,7},{6,4},{7,5},{8,10},{9,11},{10,... | collective-permute-start | bytes 313352 | tf_op jit(solution)/shard_map/ppermute | solution.py:202
  24.2 8.6 %collective-permute-start.2 = (bf16[24,2176]{1,0:T(8,128)(2,1)S(1)}, bf16[24,2176]{1,0:T(8,128)(2,1)S(1)}, u32[]{:S(2)}, u32[]{:S(2)}) collective-permute-start(bf16[24,2176]{1,0:T(8,128)(2,1)S(1)} %get-tuple-element.21), channel_id=1, source_target_pairs={{0,3},{1,2},{2,1},{3,0},{4,7},{5,6},{6,5},{7,4},{8,11},{9,10},{10,... | collective-permute-start | bytes 313352 | tf_op jit(solution)/shard_map/ppermute | solution.py:202
  33.3 11.2 %collective-permute-start.6 = (bf16[80,2176]{1,0:T(8,128)(2,1)S(1)}, bf16[80,2176]{1,0:T(8,128)(2,1)S(1)}, u32[]{:S(2)}, u32[]{:S(2)}) collective-permute-start(bf16[80,2176]{1,0:T(8,128)(2,1)S(1)} %get-tuple-element.22.pq_ref), channel_id=1, source_target_pairs={{0,8},{4,12},{8,0},{12,4},{16,24},{20,28},{24,16},{28,20},{1,9},{5... | collective-permute-start | bytes 1044488 | tf_op jit(solution)/shard_map/ppermute | solution.py:202
  35.2 20.7 %collective-permute-start.8 = (bf16[80,2176]{1,0:T(8,128)(2,1)S(1)}, bf16[80,2176]{1,0:T(8,128)(2,1)S(1)}, u32[]{:S(2)}, u32[]{:S(2)}) collective-permute-start(bf16[80,2176]{1,0:T(8,128)(2,1)S(1)} %get-tuple-element.22.pq_ref), channel_id=1, source_target_pairs={{0,16},{4,20},{8,24},{12,28},{16,0},{20,4},{24,8},{28,12},{1,17},{... | collective-permute-start | bytes 1044488 | tf_op jit(solution)/shard_map/ppermute | solution.py:202
  36.9 7.5 %copy-start.2 = (s32[4]{0:T(128)S(1)}, s32[4]{0:T(128)}, u32[]{:S(2)}) copy-start(s32[4]{0:T(128)} %len_ref.7) | copy-start | bytes 52
  36.9 30.2 %collective-permute-start.10 = (bf16[80,2176]{1,0:T(8,128)(2,1)S(1)}, bf16[80,2176]{1,0:T(8,128)(2,1)S(1)}, u32[]{:S(2)}, u32[]{:S(2)}) collective-permute-start(bf16[80,2176]{1,0:T(8,128)(2,1)S(1)} %get-tuple-element.22.pq_ref), channel_id=1, source_target_pairs={{0,24},{4,28},{8,16},{12,20},{16,8},{20,12},{24,0},{28,4},{1,25},{... | collective-permute-start | bytes 1044488 | tf_op jit(solution)/shard_map/ppermute | solution.py:202
  54.6 35.1 %collective-permute-start.7 = (bf16[80,2176]{1,0:T(8,128)(2,1)S(1)}, bf16[80,2176]{1,0:T(8,128)(2,1)S(1)}, u32[]{:S(2)}, u32[]{:S(2)}) collective-permute-start(bf16[80,2176]{1,0:T(8,128)(2,1)S(1)} %flash.5), channel_id=1, source_target_pairs={{0,8},{4,12},{8,0},{12,4},{16,24},{20,28},{24,16},{28,20},{1,9},{5... | collective-permute-start | bytes 1044488 | tf_op jit(solution)/shard_map/ppermute | solution.py:202
  66.1 23.7 %collective-permute-start.9 = (bf16[80,2176]{1,0:T(8,128)(2,1)S(1)}, bf16[80,2176]{1,0:T(8,128)(2,1)S(1)}, u32[]{:S(2)}, u32[]{:S(2)}) collective-permute-start(bf16[80,2176]{1,0:T(8,128)(2,1)S(1)} %flash.6), channel_id=1, source_target_pairs={{0,16},{4,20},{8,24},{12,28},{16,0},{20,4},{24,8},{28,12},{1,17},{... | collective-permute-start | bytes 1044488 | tf_op jit(solution)/shard_map/ppermute | solution.py:202
  77.3 12.5 %collective-permute-start.11 = (bf16[80,2176]{1,0:T(8,128)(2,1)S(1)}, bf16[80,2176]{1,0:T(8,128)(2,1)S(1)}, u32[]{:S(2)}, u32[]{:S(2)}) collective-permute-start(bf16[80,2176]{1,0:T(8,128)(2,1)S(1)} %flash.7), channel_id=1, source_target_pairs={{0,24},{4,28},{8,16},{12,20},{16,8},{20,12},{24,0},{28,4},{1,25},{... | collective-permute-start | bytes 1044488 | tf_op jit(solution)/shard_map/ppermute | solution.py:202
  90.9 4.7 %collective-permute-start.12 = (bf16[24,2048]{1,0:T(8,128)(2,1)S(1)}, bf16[24,2048]{1,0:T(8,128)(2,1)S(1)}, u32[]{:S(2)}, u32[]{:S(2)}) collective-permute-start(bf16[24,2048]{1,0:T(8,128)(2,1)S(1)} %get-tuple-element.27), channel_id=1, source_target_pairs={{0,1},{1,0},{2,3},{3,2},{4,5},{5,4},{6,7},{7,6},{8,9},{9,8},{10,11... | collective-permute-start | bytes 294920 | tf_op jit(solution)/shard_map/ppermute | solution.py:202
  91.0 5.7 %collective-permute-start.13 = (bf16[24,2048]{1,0:T(8,128)(2,1)S(1)}, bf16[24,2048]{1,0:T(8,128)(2,1)S(1)}, u32[]{:S(2)}, u32[]{:S(2)}) collective-permute-start(bf16[24,2048]{1,0:T(8,128)(2,1)S(1)} %get-tuple-element.28), channel_id=1, source_target_pairs={{0,2},{1,3},{2,0},{3,1},{4,6},{5,7},{6,4},{7,5},{8,10},{9,11},{10,... | collective-permute-start | bytes 294920 | tf_op jit(solution)/shard_map/ppermute | solution.py:202
  91.1 8.0 %collective-permute-start.14 = (bf16[24,2048]{1,0:T(8,128)(2,1)S(1)}, bf16[24,2048]{1,0:T(8,128)(2,1)S(1)}, u32[]{:S(2)}, u32[]{:S(2)}) collective-permute-start(bf16[24,2048]{1,0:T(8,128)(2,1)S(1)} %get-tuple-element.29), channel_id=1, source_target_pairs={{0,3},{1,2},{2,1},{3,0},{4,7},{5,6},{6,5},{7,4},{8,11},{9,10},{10,... | collective-permute-start | bytes 294920 | tf_op jit(solution)/shard_map/ppermute | solution.py:202

commit v2 on v1

--- a/solution.py
+++ b/solution.py
@@ -12,7 +12,6 @@
 HD = 128
 WIDE = H * HD
 META = 128
-BALANCE = True
 LOW = -1e30
 SCALE = HD**-0.5
 EXP_SCALE = SCALE * math.log2(math.e)
@@ -34,7 +33,7 @@
     return jnp.transpose(jnp.broadcast_to(column, (column.shape[0], 128)), (1, 0))[:1, :]
 
 
-def call(body, out_shape, in_specs, name, scratch=(), limit=32, cost=None):
+def call(body, out_shape, in_specs, name, scratch=(), limit=32, cost=None, aliases=None):
     many = isinstance(out_shape, list)
     return pl.pallas_call(
         body,
@@ -44,6 +43,7 @@
         scratch_shapes=list(scratch),
         compiler_params=pltpu.CompilerParams(vmem_limit_bytes=limit << 20),
         cost_estimate=cost,
+        input_output_aliases=aliases or {},
         name=name,
     )
 
@@ -92,15 +92,16 @@
     out[...] = dot(place, joined).astype(jnp.bfloat16)
 
 
-def keys_kernel(*refs):
-    pieces, k_ref, vt_ref = refs[:-2], refs[-2], refs[-1]
+def keys_kernel(first, count, *refs):
+    pieces, k_ref, vt_ref = refs[:count], refs[-2], refs[-1]
     piece = pieces[0].shape[0]
-    for i, ref in enumerate(pieces):
-        k_ref[i * piece : (i + 1) * piece, :] = ref[:, :HD]
-        vt_ref[:HD, i * piece : (i + 1) * piece] = jnp.transpose(ref[:, HD:], (1, 0))
     extra = vt_ref.shape[0] - HD
-    ones = (iota((extra, vt_ref.shape[1]), 0) == 0).astype(jnp.bfloat16)
-    vt_ref[HD:, :] = ones
+    ones = (iota((extra, piece), 0) == 0).astype(jnp.bfloat16)
+    for i, ref in enumerate(pieces, first):
+        at = slice(i * piece, (i + 1) * piece)
+        k_ref[at, :] = ref[:, :HD]
+        vt_ref[:HD, at] = jnp.transpose(ref[:, HD:], (1, 0))
+        vt_ref[HD:, at] = ones
 
 
 def flash_kernel(pieces, piece, step, info_ref, len_ref, pq_ref, k_ref, vt_ref, out_ref, acc_ref, q_ref):
@@ -218,6 +219,11 @@
     me = jnp.stack([here, mine]).astype(jnp.int32)
     bf = lambda *shape: jax.ShapeDtypeStruct(shape, jnp.bfloat16)
 
+    span = cache[0]
+    other = cycle - 2
+    kept, away = span[:half], span[half:]
+    away = swapped(away, "ctx", other)
+
     *sends, back_tok = call(
         functools.partial(route_kernel, block),
         [bf(block, wide)] * groups + [bf(tok_rows, groups * block)],
@@ -225,53 +231,75 @@
         "route",
     )(me, req_of, q_pos.reshape(1, tok_rows), queries)
     blocks = [sends[0]] + [swapped(sends[d], "req", d) for d in range(1, groups)]
-
-    span = cache[0]
-    other = cycle - 2
-    kept, away = span[:half], span[half:]
-    chip = here // 2
-    if BALANCE:
-        away = swapped(away, "ctx", other)
-        partner = here ^ other
-    else:
-        partner = here
-    kept_sib, away_sib = swapped(kept, "ctx", 1), swapped(away, "ctx", 1)
-    pieces = [kept, kept_sib, away, away_sib]
-    starts = jnp.stack(
-        [here * shard_len, (here ^ 1) * shard_len, partner * shard_len + half, (partner ^ 1) * shard_len + half]
-    ).astype(jnp.int32)
-    order = jnp.sum(starts[None, :] < starts[:, None], axis=1)
-    onehot = order[None, :] == jnp.arange(4)[:, None]
-    info = jnp.concatenate(
-        [
-            jnp.sum(jnp.where(onehot, starts[None, :], 0), axis=1),
-            jnp.sum(jnp.where(onehot, jnp.arange(4)[None, :], 0), axis=1),
-            mine[None],
-        ]
-    ).astype(jnp.int32)
-    keys = 4 * half
-    k_all, vt_all = call(keys_kernel, [bf(keys, HD), bf(HD + 16, keys)], [VMEM] * 4, "keys")(*pieces)
+    kept, blocks[0] = lax.optimization_barrier((kept, blocks[0]))
+    kept_sib = swapped(kept, "ctx", 1)
+    all_keys = [bf(4 * half, HD), bf(HD + 16, 4 * half)]
+    first = call(functools.partial(keys_kernel, 0, 2), all_keys, [VMEM] * 2, "keys_kept")(kept, kept_sib)
 
     sorted_q, back_slot = call(
         sort_kernel, [bf(slots, wide), bf(groups * block, slots)], [VMEM] * groups, "sort"
     )(*blocks)
-    visiting = [sorted_q] + [swapped(sorted_q, "ctx", 2 * d) for d in range(1, chips)]
-
-    flash = call(
-        functools.partial(flash_kernel, 4, half, 384),
-        bf(slots, wide),
-        [SMEM, SMEM] + [VMEM] * 3,
-        "flash",
-        scratch=[pltpu.VMEM((HD + 16, 512), jnp.float32), pltpu.VMEM((512, HD), jnp.bfloat16)],
-        limit=48,
-        cost=pl.CostEstimate(
-            flops=4 * slots * H * keys * HD, bytes_accessed=keys * 512, transcendentals=slots * H * keys
-        ),
-    )
-    parts = [flash(info, cache_len, q, k_all, vt_all) for q in visiting]
-    home = [parts[0]] + [swapped(parts[d], "ctx", 2 * d) for d in range(1, chips)]
+    near = [swapped(sorted_q, "ctx", 2 * d) for d in range(1, chips) if d & (d - 1) == 0]
+    mine_first, away = lax.optimization_barrier((sorted_q, away))
+
+    def key_info(starts, first=0):
+        count = len(starts)
+        starts = jnp.stack(starts).astype(jnp.int32)
+        order = jnp.sum(starts[None, :] < starts[:, None], axis=1)
+        onehot = order[None, :] == jnp.arange(count)[:, None]
+        return jnp.concatenate(
+            [
+                jnp.sum(jnp.where(onehot, starts[None, :], 0), axis=1),
+                first + jnp.sum(jnp.where(onehot, jnp.arange(count)[None, :], 0), axis=1),
+                mine[None],
+            ]
+        ).astype(jnp.int32)
+
+    def flash(info, q, k, vt):
+        pieces = info.shape[0] // 2
+        keys = pieces * half
+        return call(
+            functools.partial(flash_kernel, pieces, half, 384),
+            bf(slots, wide),
+            [SMEM, SMEM] + [VMEM] * 3,
+            "flash",
+            scratch=[pltpu.VMEM((HD + 16, 512), jnp.float32), pltpu.VMEM((512, HD), jnp.bfloat16)],
+            limit=48,
+            cost=pl.CostEstimate(
+                flops=4 * slots * H * keys * HD, bytes_accessed=keys * 512, transcendentals=slots * H * keys
+            ),
+        )(info, cache_len, q, k, vt)
+
+    partner = here ^ other
+    kept_at = [here * shard_len, (here ^ 1) * shard_len]
+    away_at = [partner * shard_len + half, (partner ^ 1) * shard_len + half]
+    own_kept = flash(key_info(kept_at), mine_first, *first)
+    away_sib = swapped(away, "ctx", 1)
+    own_kept, *first = lax.optimization_barrier((own_kept, *first))
+    k_all, vt_all = call(
+        functools.partial(keys_kernel, 2, 2), all_keys, [VMEM] * 4, "keys_away", aliases={2: 0, 3: 1}
+    )(away, away_sib, *first)
+    info = key_info(kept_at + away_at)
+    far = [swapped(sorted_q, "ctx", 2 * d) for d in range(1, chips) if d & (d - 1) != 0]
+    turn = own_kept
+    parts = {}
+    waiting = dict(zip([d for d in range(1, chips) if d & (d - 1) == 0], near))
+    waiting.update(zip([d for d in range(1, chips) if d & (d - 1) != 0], far))
+    for d in waiting:
+        turn, q = lax.optimization_barrier((turn, waiting[d]))
+        if d == 1:
+            own_kept = turn
+        else:
+            parts[before] = turn
+        turn = flash(info, q, k_all, vt_all)
+        before = d
+    parts[before] = turn
+    home = [swapped(parts[d], "ctx", 2 * d) for d in parts]
+    last, q = lax.optimization_barrier((turn, sorted_q))
+    own_away = flash(key_info(away_at, 2), q, k_all, vt_all)
+    home += [own_kept, own_away]
     outs = call(
-        functools.partial(merge_kernel, chips), [bf(block, WIDE)] * groups, [VMEM] * (chips + 1), "merge"
+        functools.partial(merge_kernel, chips + 1), [bf(block, WIDE)] * groups, [VMEM] * (chips + 2), "merge"
     )(*home, back_slot)
     back = [outs[0]] + [swapped(outs[d], "req", d) for d in range(1, groups)]
     return call(unroute_kernel, bf(tok_rows, WIDE), [VMEM] * (groups + 1), "unroute")(*back, back_tok)

time: 100 us -> 98.9 us (0.989)
  Pallas kernels: 44.8 us -> 23.1 us
  starting transfers between devices: 21 us -> 34.9 us
  waiting for transfers between devices: 32.1 us -> 35.3 us
  local copies, waits for them, and re-layouts: 1.47 us -> 3.67 us
    pallas_call x6 -> x8, Pallas kernels: 42.4 us -> 20.8 us  [the longest x5 19 us: flash(): call(functools.partial(flash_kernel, pieces, half, 384), bf(slots, wide),...]
    ppermute x15, starting transfers between devices: 21 us -> 34.9 us  [swapped(): return lax.ppermute(block, axis, [(i, i ^ distance) for i in devices])]
    ppermute x15, waiting for transfers between devices: 32.1 us -> 35.3 us  [swapped(): return lax.ppermute(block, axis, [(i, i ^ distance) for i in devices])]
    unnamed x9 -> x7, local copies, waits for them, and re-layouts: 0.11 us -> 2.35 us
  transfers between devices with their start and end apart: 15 -> 15, of which waited for: 7 -> 7; matrix products, arithmetic and copies ran while one was open for 1% -> 3% of each run, Pallas kernels for 43% -> 16%
where the time goes in v2:
time: 98.9 us; the launch traced here: 98.6 us
  waiting for transfers between devices  35.3 us (36%)
  starting transfers between devices  34.9 us (35%)
  Pallas kernels  23.1 us (23%)
  local copies, waits for them, and re-layouts  3.67 us (4%)
  other arithmetic  1.53 us (2%)
    ppermute x15, waiting for transfers between devices, swapped(): return lax.ppermute(block, axis, [(i, i ^ distance) for i in devices])  35.3 us
    ppermute x15, starting transfers between devices, swapped(): return lax.ppermute(block, axis, [(i, i ^ distance) for i in devices])  34.9 us
    pallas_call x5, Pallas kernels, flash(): call(functools.partial(flash_kernel, pieces, half, 384), bf(slots, wide),...  19 us
    unnamed x7, local copies, waits for them, and re-layouts  2.35 us
  transfers between devices with their start and end apart: 15, of which 7 were waited for; matrix products, arithmetic and copies ran while one was open for 3% of the time, Pallas kernels for 16%

profile of v2, /device:TPU:0, one launch (start us, length us, event | category | flops | bytes accessed | tf_op | source)
XLA Modules:
  0.0 98.6 jit_solution(8637829291091946222)
XLA Ops:
  0.0 0.7 copy.9.req_ref
  0.8 0.9 copy-done
  1.8 0.7 copy-done.1
  2.4 0.9 route.1
  3.4 3.1 %collective-permute-start = (bf16[24,2176]{1,0:T(8,128)(2,1)S(1)}, bf16[24,2176]{1,0:T(8,128)(2,1)S(1)}, u32[]{:S(2)}, u32[]{:S(2)}) collective-permute-start(bf16[24,2176]{1,0:T(8,128)(2,1)S(1)} %get-tuple-element.36), channel_id=1, source_target_pairs={{0,1},{1,0},{2,3},{3,2},{4,5},{5,4},{6,7},{7,6},{8,9},{9,8},{10,11... | collective-permute-start | bytes 313352 | tf_op jit(solution)/shard_map/ppermute | solution.py:203
  6.5 2.6 %collective-permute-start.1 = (bf16[24,2176]{1,0:T(8,128)(2,1)S(1)}, bf16[24,2176]{1,0:T(8,128)(2,1)S(1)}, u32[]{:S(2)}, u32[]{:S(2)}) collective-permute-start(bf16[24,2176]{1,0:T(8,128)(2,1)S(1)} %get-tuple-element.37), channel_id=1, source_target_pairs={{0,2},{1,3},{2,0},{3,1},{4,6},{5,7},{6,4},{7,5},{8,10},{9,11},{10,... | collective-permute-start | bytes 313352 | tf_op jit(solution)/shard_map/ppermute | solution.py:203
  9.1 1.3 %slice_bitcast_fusion = (bf16[1152,256]{1,0:T(8,128)(2,1)S(1)}, bf16[1152,256]{1,0:T(8,128)(2,1)S(1)}) fusion(bf16[1,2304,256]{2,1,0:T(8,128)(2,1)} %param.8), kind=kLoop, calls=%fused_computation | loop fusion | bytes 2359296 | tf_op jit(solution)/shard_map/slice | solution.py:224
  10.4 2.7 %collective-permute-start.3 = (bf16[1152,256]{1,0:T(8,128)(2,1)S(1)}, bf16[1152,256]{1,0:T(8,128)(2,1)S(1)}, u32[]{:S(2)}, u32[]{:S(2)}) collective-permute-start(bf16[1152,256]{1,0:T(8,128)(2,1)S(1)} %get-tuple-element.69), channel_id=1, source_target_pairs={{0,24},{4,28},{8,16},{12,20},{16,8},{20,12},{24,0},{28,4},{1,25},{... | collective-permute-start | bytes 1769480 | tf_op jit(solution)/shard_map/ppermute | solution.py:203
  13.3 0.2 fusion
  14.0 3.3 %collective-permute-done.1.refs_2_ = bf16[24,2176]{1,0:T(8,128)(2,1)S(1)} collective-permute-done((bf16[24,2176]{1,0:T(8,128)(2,1)S(1)}, bf16[24,2176]{1,0:T(8,128)(2,1)S(1)}, u32[]{:S(2)}, u32[]{:S(2)}) %collective-permute-start.1) | collective-permute-done | bytes 104480 | tf_op jit(solution)/shard_map/ppermute | solution.py:203
  17.3 0.5 sort.1
  17.8 8.0 %collective-permute-done.3.refs_0_ = bf16[1152,256]{1,0:T(8,128)(2,1)S(1)} collective-permute-done((bf16[1152,256]{1,0:T(8,128)(2,1)S(1)}, bf16[1152,256]{1,0:T(8,128)(2,1)S(1)}, u32[]{:S(2)}, u32[]{:S(2)}) %collective-permute-start.3) | collective-permute-done | bytes 589856 | tf_op jit(solution)/shard_map/ppermute | solution.py:203
  26.1 1.6 %collective-permute-start.5 = (bf16[80,2176]{1,0:T(8,128)(2,1)S(1)}, bf16[80,2176]{1,0:T(8,128)(2,1)S(1)}, u32[]{:S(2)}, u32[]{:S(2)}) collective-permute-start(bf16[80,2176]{1,0:T(8,128)(2,1)S(1)} %get-tuple-element.56.pq_ref), channel_id=1, source_target_pairs={{0,8},{4,12},{8,0},{12,4},{16,24},{20,28},{24,16},{28,20},{1,9},{5... | collective-permute-start | bytes 1044488 | tf_op jit(solution)/shard_map/ppermute | solution.py:203
  27.9 1.6 %collective-permute-start.7 = (bf16[80,2176]{1,0:T(8,128)(2,1)S(1)}, bf16[80,2176]{1,0:T(8,128)(2,1)S(1)}, u32[]{:S(2)}, u32[]{:S(2)}) collective-permute-start(bf16[80,2176]{1,0:T(8,128)(2,1)S(1)} %get-tuple-element.56.pq_ref), channel_id=1, source_target_pairs={{0,16},{4,20},{8,24},{12,28},{16,0},{20,4},{24,8},{28,12},{1,17},{... | collective-permute-start | bytes 1044488 | tf_op jit(solution)/shard_map/ppermute | solution.py:203
  29.5 0.5 collective-permute-start.9
  30.0 0.2 keys_kept.1
  30.2 4.2 %flash.5.refs_3_ = bf16[80,2176]{1,0:T(8,128)(2,1)S(1)} custom-call(s32[5]{0:T(128)S(1)} %add_add_fusion.info_ref, s32[4]{0:T(128)S(1)} %copy-done.2, bf16[80,2176]{1,0:T(8,128)(2,1)S(1)} %get-tuple-element.56.pq_ref, bf16[4608,128]{1,0:T(8,128)(2,1)S(1)} %get-tuple-element.47.k_ref.refs_2_, bf16[144,4608]{1,0:T(8,128)(2,1)S(1)} %get-tuple-element.48.vt_ref.refs_3_), custom_call_target="tpu_custom_call" | custom-call | flops 1509949440 | bytes 1179648 | tf_op jit(solution)/shard_map/flash/pallas_call | solution.py:261
  34.5 2.7 %collective-permute-done.5.pq_ref = bf16[80,2176]{1,0:T(8,128)(2,1)S(1)} collective-permute-done((bf16[80,2176]{1,0:T(8,128)(2,1)S(1)}, bf16[80,2176]{1,0:T(8,128)(2,1)S(1)}, u32[]{:S(2)}, u32[]{:S(2)}) %collective-permute-start.5) | collective-permute-done | bytes 348192 | tf_op jit(solution)/shard_map/ppermute | solution.py:203
  37.1 0.2 keys_away.1
  37.4 4.2 %flash.6 = bf16[80,2176]{1,0:T(8,128)(2,1)S(1)} custom-call(s32[9]{0:T(128)S(1)} %pad_add_fusion.1.info_ref, s32[4]{0:T(128)S(1)} %copy-done.2, bf16[80,2176]{1,0:T(8,128)(2,1)S(1)} %collective-permute-done.5.pq_ref, bf16[4608,128]{1,0:T(8,128)(2,1)S(1)} %get-tuple-element.49.k_ref, bf16[144,4608]{1,0:T(8,128)(2,1)S(1)} %get-tuple-element.50.vt_ref), custom_call_target="tpu_custom_call" | custom-call | flops 3019898880 | bytes 2359296 | tf_op jit(solution)/shard_map/flash/pallas_call | solution.py:261
  41.6 4.1 %collective-permute-done.7.pq_ref = bf16[80,2176]{1,0:T(8,128)(2,1)S(1)} collective-permute-done((bf16[80,2176]{1,0:T(8,128)(2,1)S(1)}, bf16[80,2176]{1,0:T(8,128)(2,1)S(1)}, u32[]{:S(2)}, u32[]{:S(2)}) %collective-permute-start.7) | collective-permute-done | bytes 348192 | tf_op jit(solution)/shard_map/ppermute | solution.py:203
  45.7 4.3 %flash.7 = bf16[80,2176]{1,0:T(8,128)(2,1)S(1)} custom-call(s32[9]{0:T(128)S(1)} %pad_add_fusion.1.info_ref, s32[4]{0:T(128)S(1)} %copy-done.2, bf16[80,2176]{1,0:T(8,128)(2,1)S(1)} %collective-permute-done.7.pq_ref, bf16[4608,128]{1,0:T(8,128)(2,1)S(1)} %get-tuple-element.49.k_ref, bf16[144,4608]{1,0:T(8,128)(2,1)S(1)} %get-tuple-element.50.vt_ref), custom_call_target="tpu_custom_call" | custom-call | flops 3019898880 | bytes 2359296 | tf_op jit(solution)/shard_map/flash/pallas_call | solution.py:261
  50.0 4.2 %flash.8 = bf16[80,2176]{1,0:T(8,128)(2,1)S(1)} custom-call(s32[9]{0:T(128)S(1)} %pad_add_fusion.1.info_ref, s32[4]{0:T(128)S(1)} %copy-done.2, bf16[80,2176]{1,0:T(8,128)(2,1)S(1)} %collective-permute-done.9.pq_ref, bf16[4608,128]{1,0:T(8,128)(2,1)S(1)} %get-tuple-element.49.k_ref, bf16[144,4608]{1,0:T(8,128)(2,1)S(1)} %get-tuple-element.50.vt_ref), custom_call_target="tpu_custom_call" | custom-call | flops 3019898880 | bytes 2359296 | tf_op jit(solution)/shard_map/flash/pallas_call | solution.py:261
  54.4 3.4 %collective-permute-start.8 = (bf16[80,2176]{1,0:T(8,128)(2,1)S(1)}, bf16[80,2176]{1,0:T(8,128)(2,1)S(1)}, u32[]{:S(2)}, u32[]{:S(2)}) collective-permute-start(bf16[80,2176]{1,0:T(8,128)(2,1)S(1)} %flash.6), channel_id=1, source_target_pairs={{0,8},{4,12},{8,0},{12,4},{16,24},{20,28},{24,16},{28,20},{1,9},{5... | collective-permute-start | bytes 1044488 | tf_op jit(solution)/shard_map/ppermute | solution.py:203
  57.9 2.0 %flash.9.refs_4_ = bf16[80,2176]{1,0:T(8,128)(2,1)S(1)} custom-call(s32[5]{0:T(128)S(1)} %add_add_fusion.1.info_ref, s32[4]{0:T(128)S(1)} %copy-done.2, bf16[80,2176]{1,0:T(8,128)(2,1)S(1)} %get-tuple-element.56.pq_ref, bf16[4608,128]{1,0:T(8,128)(2,1)S(1)} %get-tuple-element.49.k_ref, bf16[144,4608]{1,0:T(8,128)(2,1)S(1)} %get-tuple-element.50.vt_ref), custom_call_target="tpu_custom_call" | custom-call | flops 1509949440 | bytes 1179648 | tf_op jit(solution)/shard_map/flash/pallas_call | solution.py:261
  59.8 6.4 %collective-permute-done.11.refs_2_ = bf16[80,2176]{1,0:T(8,128)(2,1)S(1)} collective-permute-done((bf16[80,2176]{1,0:T(8,128)(2,1)S(1)}, bf16[80,2176]{1,0:T(8,128)(2,1)S(1)}, u32[]{:S(2)}, u32[]{:S(2)}) %collective-permute-start.11) | collective-permute-done | bytes 348192 | tf_op jit(solution)/shard_map/ppermute | solution.py:203
  66.3 4.0 %collective-permute-done.10.refs_1_ = bf16[80,2176]{1,0:T(8,128)(2,1)S(1)} collective-permute-done((bf16[80,2176]{1,0:T(8,128)(2,1)S(1)}, bf16[80,2176]{1,0:T(8,128)(2,1)S(1)}, u32[]{:S(2)}, u32[]{:S(2)}) %collective-permute-start.10) | collective-permute-done | bytes 348192 | tf_op jit(solution)/shard_map/ppermute | solution.py:203
  70.2 1.4 %merge.1 = (bf16[24,2048]{1,0:T(8,128)(2,1)S(1)}, bf16[24,2048]{1,0:T(8,128)(2,1)S(1)}, bf16[24,2048]{1,0:T(8,128)(2,1)S(1)}, bf16[24,2048]{1,0:T(8,128)(2,1)S(1)}) custom-call(bf16[80,2176]{1,0:T(8,128)(2,1)S(1)} %collective-permute-done.8.refs_0_, bf16[80,2176]{1,0:T(8,128)(2,1)S(1)} %collective-permute-done.10.refs_1_, ...), custom_call_target="tpu_custom_call" | custom-call | tf_op jit(solution)/shard_map/merge/pallas_call | solution.py:301
  71.6 12.1 %collective-permute-start.12 = (bf16[24,2048]{1,0:T(8,128)(2,1)S(1)}, bf16[24,2048]{1,0:T(8,128)(2,1)S(1)}, u32[]{:S(2)}, u32[]{:S(2)}) collective-permute-start(bf16[24,2048]{1,0:T(8,128)(2,1)S(1)} %get-tuple-element.59), channel_id=1, source_target_pairs={{0,1},{1,0},{2,3},{3,2},{4,5},{5,4},{6,7},{7,6},{8,9},{9,8},{10,11... | collective-permute-start | bytes 294920 | tf_op jit(solution)/shard_map/ppermute | solution.py:203
  83.7 7.1 %collective-permute-start.13 = (bf16[24,2048]{1,0:T(8,128)(2,1)S(1)}, bf16[24,2048]{1,0:T(8,128)(2,1)S(1)}, u32[]{:S(2)}, u32[]{:S(2)}) collective-permute-start(bf16[24,2048]{1,0:T(8,128)(2,1)S(1)} %get-tuple-element.60), channel_id=1, source_target_pairs={{0,2},{1,3},{2,0},{3,1},{4,6},{5,7},{6,4},{7,5},{8,10},{9,11},{10,... | collective-permute-start | bytes 294920 | tf_op jit(solution)/shard_map/ppermute | solution.py:203
  90.9 6.8 %collective-permute-done.13.refs_2_ = bf16[24,2048]{1,0:T(8,128)(2,1)S(1)} collective-permute-done((bf16[24,2048]{1,0:T(8,128)(2,1)S(1)}, bf16[24,2048]{1,0:T(8,128)(2,1)S(1)}, u32[]{:S(2)}, u32[]{:S(2)}) %collective-permute-start.13) | collective-permute-done | bytes 98336 | tf_op jit(solution)/shard_map/ppermute | solution.py:203
  97.7 0.9 unroute.1
  (31 shorter events, 1.6 us)
Async XLA Ops:
  0.8 0.9 copy-start
  1.8 0.7 copy-start.1
  3.4 10.7 %collective-permute-start = (bf16[24,2176]{1,0:T(8,128)(2,1)S(1)}, bf16[24,2176]{1,0:T(8,128)(2,1)S(1)}, u32[]{:S(2)}, u32[]{:S(2)}) collective-permute-start(bf16[24,2176]{1,0:T(8,128)(2,1)S(1)} %get-tuple-element.36), channel_id=1, source_target_pairs={{0,1},{1,0},{2,3},{3,2},{4,5},{5,4},{6,7},{7,6},{8,9},{9,8},{10,11... | collective-permute-start | bytes 313352 | tf_op jit(solution)/shard_map/ppermute | solution.py:203
  6.5 10.9 %collective-permute-start.1 = (bf16[24,2176]{1,0:T(8,128)(2,1)S(1)}, bf16[24,2176]{1,0:T(8,128)(2,1)S(1)}, u32[]{:S(2)}, u32[]{:S(2)}) collective-permute-start(bf16[24,2176]{1,0:T(8,128)(2,1)S(1)} %get-tuple-element.37), channel_id=1, source_target_pairs={{0,2},{1,3},{2,0},{3,1},{4,6},{5,7},{6,4},{7,5},{8,10},{9,11},{10,... | collective-permute-start | bytes 313352 | tf_op jit(solution)/shard_map/ppermute | solution.py:203
  9.1 8.3 %collective-permute-start.2 = (bf16[24,2176]{1,0:T(8,128)(2,1)S(1)}, bf16[24,2176]{1,0:T(8,128)(2,1)S(1)}, u32[]{:S(2)}, u32[]{:S(2)}) collective-permute-start(bf16[24,2176]{1,0:T(8,128)(2,1)S(1)} %get-tuple-element.38), channel_id=1, source_target_pairs={{0,3},{1,2},{2,1},{3,0},{4,7},{5,6},{6,5},{7,4},{8,11},{9,10},{10,... | collective-permute-start | bytes 313352 | tf_op jit(solution)/shard_map/ppermute | solution.py:203
  10.4 19.8 %copy-start.2 = (s32[4]{0:T(128)S(1)}, s32[4]{0:T(128)}, u32[]{:S(2)}) copy-start(s32[4]{0:T(128)} %len_ref.9) | copy-start | bytes 52
  10.4 15.5 %collective-permute-start.3 = (bf16[1152,256]{1,0:T(8,128)(2,1)S(1)}, bf16[1152,256]{1,0:T(8,128)(2,1)S(1)}, u32[]{:S(2)}, u32[]{:S(2)}) collective-permute-start(bf16[1152,256]{1,0:T(8,128)(2,1)S(1)} %get-tuple-element.69), channel_id=1, source_target_pairs={{0,24},{4,28},{8,16},{12,20},{16,8},{20,12},{24,0},{28,4},{1,25},{... | collective-permute-start | bytes 1769480 | tf_op jit(solution)/shard_map/ppermute | solution.py:203
  13.1 16.8 %collective-permute-start.4 = (bf16[1152,256]{1,0:T(8,128)(2,1)S(1)}, bf16[1152,256]{1,0:T(8,128)(2,1)S(1)}, u32[]{:S(2)}, u32[]{:S(2)}) collective-permute-start(bf16[1152,256]{1,0:T(8,128)(2,1)S(1)} %get-tuple-element.41.refs_0_), channel_id=1, source_target_pairs={{0,4},{4,0},{8,12},{12,8},{16,20},{20,16},{24,28},{28,24},{1,5},{5... | collective-permute-start | bytes 1769480 | tf_op jit(solution)/shard_map/ppermute | solution.py:203
  25.9 11.3 %collective-permute-start.6 = (bf16[1152,256]{1,0:T(8,128)(2,1)S(1)}, bf16[1152,256]{1,0:T(8,128)(2,1)S(1)}, u32[]{:S(2)}, u32[]{:S(2)}) collective-permute-start(bf16[1152,256]{1,0:T(8,128)(2,1)S(1)} %collective-permute-done.3.refs_0_), channel_id=1, source_target_pairs={{0,4},{4,0},{8,12},{12,8},{16,20},{20,16},{24,28},{28,24},{1,5},{5... | collective-permute-start | bytes 1769480 | tf_op jit(solution)/shard_map/ppermute | solution.py:203
  26.1 11.0 %collective-permute-start.5 = (bf16[80,2176]{1,0:T(8,128)(2,1)S(1)}, bf16[80,2176]{1,0:T(8,128)(2,1)S(1)}, u32[]{:S(2)}, u32[]{:S(2)}) collective-permute-start(bf16[80,2176]{1,0:T(8,128)(2,1)S(1)} %get-tuple-element.56.pq_ref), channel_id=1, source_target_pairs={{0,8},{4,12},{8,0},{12,4},{16,24},{20,28},{24,16},{28,20},{1,9},{5... | collective-permute-start | bytes 1044488 | tf_op jit(solution)/shard_map/ppermute | solution.py:203
  27.9 17.8 %collective-permute-start.7 = (bf16[80,2176]{1,0:T(8,128)(2,1)S(1)}, bf16[80,2176]{1,0:T(8,128)(2,1)S(1)}, u32[]{:S(2)}, u32[]{:S(2)}) collective-permute-start(bf16[80,2176]{1,0:T(8,128)(2,1)S(1)} %get-tuple-element.56.pq_ref), channel_id=1, source_target_pairs={{0,16},{4,20},{8,24},{12,28},{16,0},{20,4},{24,8},{28,12},{1,17},{... | collective-permute-start | bytes 1044488 | tf_op jit(solution)/shard_map/ppermute | solution.py:203
  29.5 20.5 %collective-permute-start.9 = (bf16[80,2176]{1,0:T(8,128)(2,1)S(1)}, bf16[80,2176]{1,0:T(8,128)(2,1)S(1)}, u32[]{:S(2)}, u32[]{:S(2)}) collective-permute-start(bf16[80,2176]{1,0:T(8,128)(2,1)S(1)} %get-tuple-element.56.pq_ref), channel_id=1, source_target_pairs={{0,24},{4,28},{8,16},{12,20},{16,8},{20,12},{24,0},{28,4},{1,25},{... | collective-permute-start | bytes 1044488 | tf_op jit(solution)/shard_map/ppermute | solution.py:203
  54.2 12.1 %collective-permute-start.11 = (bf16[80,2176]{1,0:T(8,128)(2,1)S(1)}, bf16[80,2176]{1,0:T(8,128)(2,1)S(1)}, u32[]{:S(2)}, u32[]{:S(2)}) collective-permute-start(bf16[80,2176]{1,0:T(8,128)(2,1)S(1)} %flash.8), channel_id=1, source_target_pairs={{0,24},{4,28},{8,16},{12,20},{16,8},{20,12},{24,0},{28,4},{1,25},{... | collective-permute-start | bytes 1044488 | tf_op jit(solution)/shard_map/ppermute | solution.py:203
  54.3 15.9 %collective-permute-start.10 = (bf16[80,2176]{1,0:T(8,128)(2,1)S(1)}, bf16[80,2176]{1,0:T(8,128)(2,1)S(1)}, u32[]{:S(2)}, u32[]{:S(2)}) collective-permute-start(bf16[80,2176]{1,0:T(8,128)(2,1)S(1)} %flash.7), channel_id=1, source_target_pairs={{0,16},{4,20},{8,24},{12,28},{16,0},{20,4},{24,8},{28,12},{1,17},{... | collective-permute-start | bytes 1044488 | tf_op jit(solution)/shard_map/ppermute | solution.py:203
  54.4 15.9 %collective-permute-start.8 = (bf16[80,2176]{1,0:T(8,128)(2,1)S(1)}, bf16[80,2176]{1,0:T(8,128)(2,1)S(1)}, u32[]{:S(2)}, u32[]{:S(2)}) collective-permute-start(bf16[80,2176]{1,0:T(8,128)(2,1)S(1)} %flash.6), channel_id=1, source_target_pairs={{0,8},{4,12},{8,0},{12,4},{16,24},{20,28},{24,16},{28,20},{1,9},{5... | collective-permute-start | bytes 1044488 | tf_op jit(solution)/shard_map/ppermute | solution.py:203
  71.6 19.3 %collective-permute-start.12 = (bf16[24,2048]{1,0:T(8,128)(2,1)S(1)}, bf16[24,2048]{1,0:T(8,128)(2,1)S(1)}, u32[]{:S(2)}, u32[]{:S(2)}) collective-permute-start(bf16[24,2048]{1,0:T(8,128)(2,1)S(1)} %get-tuple-element.59), channel_id=1, source_target_pairs={{0,1},{1,0},{2,3},{3,2},{4,5},{5,4},{6,7},{7,6},{8,9},{9,8},{10,11... | collective-permute-start | bytes 294920 | tf_op jit(solution)/shard_map/ppermute | solution.py:203
  83.7 14.0 %collective-permute-start.13 = (bf16[24,2048]{1,0:T(8,128)(2,1)S(1)}, bf16[24,2048]{1,0:T(8,128)(2,1)S(1)}, u32[]{:S(2)}, u32[]{:S(2)}) collective-permute-start(bf16[24,2048]{1,0:T(8,128)(2,1)S(1)} %get-tuple-element.60), channel_id=1, source_target_pairs={{0,2},{1,3},{2,0},{3,1},{4,6},{5,7},{6,4},{7,5},{8,10},{9,11},{10,... | collective-permute-start | bytes 294920 | tf_op jit(solution)/shard_map/ppermute | solution.py:203
  90.8 6.9 %collective-permute-start.14 = (bf16[24,2048]{1,0:T(8,128)(2,1)S(1)}, bf16[24,2048]{1,0:T(8,128)(2,1)S(1)}, u32[]{:S(2)}, u32[]{:S(2)}) collective-permute-start(bf16[24,2048]{1,0:T(8,128)(2,1)S(1)} %get-tuple-element.61), channel_id=1, source_target_pairs={{0,3},{1,2},{2,1},{3,0},{4,7},{5,6},{6,5},{7,4},{8,11},{9,10},{10,... | collective-permute-start | bytes 294920 | tf_op jit(solution)/shard_map/ppermute | solution.py:203
